TPU v7x, 128 devices: a whole 4x4x4 slice. The times are simulated.
128 devices in a mesh: grp: 2 (over core), tp: 32 (over z, x_lo, y), dp: 2 (over x_hi).
Axes of the slice: x: 4 (x_hi: 2, x_lo: 2; x = x_hi * 2 + x_lo), y: 4, z: 4, core: 2. Of those that a mesh axis runs over, the one named last changes fastest.
Arguments:
- base_inputs: bfloat16 [3, 128, 8192], P(None, 'dp', ('grp', 'tp')), may hold values from -6 to 6
- small_inputs: bfloat16 [2, 3, 128, 4096], P('grp', None, 'dp', 'tp'), may hold values from -6 to 6
- base_norm_gain: float32 [8192], replicated, may hold values from 0.1 to 1.9
- base_query: bfloat16 [8192, 8192], P(None, ('grp', 'tp')), may hold values from -0.0625 to 0.0625
- base_keys_values: bfloat16 [2, 8192, 1024], P(None, None, ('grp', 'tp')), may hold values from -0.0625 to 0.0625
- base_output: bfloat16 [8192, 8192], P(('grp', 'tp')), may hold values from -0.0625 to 0.0625
- base_cache: bfloat16 [2, 128, 1024, 128], P(None, 'dp', ('grp', 'tp')), may hold values from -600 to 600
- base_final_gain: float32 [8192], replicated, may hold values from 0.1 to 1.9
- base_unembed: bfloat16 [16384, 8192], P(('grp', 'tp')), may hold values from -20 to 20
- small_norm_gain: float32 [2, 4096], P('grp'), may hold values from 0.1 to 1.9
- small_projections: bfloat16 [2, 3, 4096, 4096], P('grp', None, None, 'tp'), may hold values from -0.09375 to 0.09375
- small_output: bfloat16 [2, 4096, 4096], P('grp', 'tp'), may hold values from -0.09375 to 0.09375
- small_cache: bfloat16 [2, 2, 128, 4096, 128], P('grp', None, 'dp', 'tp'), may hold values from -600 to 600
- small_final_gain: float32 [2, 4096], P('grp'), may hold values from 0.1 to 1.9
- small_unembed: bfloat16 [2, 2, 8192, 4096], P('grp', None, 'tp'), may hold values from -0.1875 to 0.1875
- lengths: int32 [128], P('dp'), may hold values from 1 to 128, as said below
- next_tokens: int32 [3, 128], P(None, 'dp'), may hold values from 0 to 16383
Outputs:
- log_probs: float32 [3, 128, 16384], P(None, 'dp', ('grp', 'tp'))
- chosen_total: float32 [128], P('dp')
Inputs may be any that keep to these rules, and one draw needn't show every extreme that they name: `lengths`: some row holds 128 cached positions.
All inputs are finite; a program needn't handle non-finite values.
Results may differ from a plain program's by a relative error of at most 0.0035.
Values may be sent and summed in bfloat16 or wider, within the bound.
No kernel may reach another device: no remote copies, remote signals or barrier semaphores. Data moves between devices by JAX's collectives and lax.ppermute only.
A program may use at most 128 MiB of HBM per device.

v0:
```python
import math

import jax
import jax.numpy as jnp
from jax import lax
from jax.sharding import PartitionSpec as P

HD = 128
STEPS = 3
CACHE = 128


EPSILON = 1e-05
NEGATIVE = -1e30


def partner(array, axis, bit):
    return lax.ppermute(array, axis, [(i, i ^ 1 << bit) for i in range(lax.axis_size(axis))])


def rotate_pairs(values, positions, first_pair, head_size):
    pair_count = values.shape[-1] // 2
    pair_index = (first_pair + jnp.arange(pair_count)).astype(jnp.float32)
    frequency = jnp.exp(pair_index * (-2.0 * math.log(10000.0) / head_size))
    angles = positions.astype(jnp.float32)[:, None] * frequency[None, :]
    angles = angles.reshape((values.shape[0],) + (1,) * (values.ndim - 2) + (pair_count,))
    cosine = jnp.cos(angles)
    sine_part = jnp.sin(angles)
    paired = values.reshape(values.shape[:-1] + (pair_count, 2))
    even_part = paired[..., 0]
    odd_part = paired[..., 1]
    turned = jnp.stack(
        [even_part * cosine - odd_part * sine_part, even_part * sine_part + odd_part * cosine],
        axis=-1,
    )
    return turned.reshape(values.shape)


def norm_rows(values, gain_row):
    values = values.astype(jnp.float32)
    scaling = lax.rsqrt(jnp.mean(values * values, axis=-1, keepdims=True) + EPSILON)
    return (values * scaling * gain_row).astype(jnp.bfloat16)


def attention_weights(cached_scores, fresh_scores, visible, head_size):
    factor = 1.0 / math.sqrt(head_size)
    cached_scores = jnp.where(visible, cached_scores * factor, NEGATIVE)
    fresh_scores = fresh_scores * factor
    row_max = jnp.maximum(
        jnp.max(cached_scores, axis=-1, keepdims=True),
        jnp.max(fresh_scores, axis=-1, keepdims=True),
    )
    cached_exp = jnp.exp(cached_scores - row_max)
    fresh_exp = jnp.exp(fresh_scores - row_max)
    totals = jnp.sum(cached_exp, axis=-1, keepdims=True) + jnp.sum(
        fresh_exp, axis=-1, keepdims=True
    )
    return ((cached_exp / totals).astype(jnp.bfloat16), (fresh_exp / totals).astype(jnp.bfloat16))


def sum_slices(scores, share_count):
    for bit_index in range(share_count.bit_length() - 1):
        scores = scores + partner(scores, "tp", bit_index)
    return scores


def body(
    base_inputs,
    small_inputs,
    base_norm_gain,
    base_query,
    base_keys_values,
    base_output,
    base_cache,
    base_final_gain,
    base_unembed,
    small_norm_gain,
    small_projections,
    small_output,
    small_cache,
    small_final_gain,
    small_unembed,
    lengths,
    next_tokens,
):
    row_count = lengths.shape[0]
    slice_width = base_keys_values.shape[2]
    share_count = HD // slice_width
    group_size = base_query.shape[1] // slice_width
    slice_index = lax.axis_index("tp") % share_count
    first_pair = slice_index * (slice_width // 2)
    block_index = lax.axis_index(("grp", "tp"))
    vocab_width = base_unembed.shape[0]
    small_heads = small_projections.shape[3] // HD
    base_full = lax.all_gather(base_inputs, ("grp", "tp"), axis=2, tiled=True)
    small_full = lax.all_gather(small_inputs[0], "tp", axis=2, tiled=True)
    visible = (jnp.arange(CACHE)[None, :] < lengths[:, None])[:, None, :]
    base_keys_cache = base_cache[0]
    base_values_cache = base_cache[1]
    small_keys_cache = small_cache[0, 0].reshape(row_count, small_heads, HD, CACHE)
    small_values_cache = small_cache[0, 1].reshape(row_count, small_heads, HD, CACHE)
    small_table = small_unembed[0].reshape(-1, small_unembed.shape[3])
    base_new_keys = []
    base_new_values = []
    small_new_keys = []
    small_new_values = []
    log_steps = []
    chosen_total = jnp.zeros((row_count,), jnp.float32)
    for step_index in range(STEPS):
        positions = lengths + step_index
        small_normed = norm_rows(small_full[step_index], small_norm_gain[0])
        small_queries = jnp.dot(
            small_normed, small_projections[0, 0], preferred_element_type=jnp.float32
        ).reshape(row_count, small_heads, HD)
        small_queries = rotate_pairs(small_queries, positions, 0, HD).astype(jnp.bfloat16)
        small_key = jnp.dot(
            small_normed, small_projections[0, 1], preferred_element_type=jnp.float32
        ).reshape(row_count, small_heads, HD)
        small_new_keys.append(rotate_pairs(small_key, positions, 0, HD).astype(jnp.bfloat16))
        small_value = jnp.dot(
            small_normed, small_projections[0, 2], preferred_element_type=jnp.float32
        ).reshape(row_count, small_heads, HD)
        small_new_values.append(small_value.astype(jnp.bfloat16))
        small_fresh_keys = jnp.stack(small_new_keys, axis=-1)
        small_fresh_values = jnp.stack(small_new_values, axis=-1)
        small_cached_scores = jnp.einsum(
            "rhd,rhdl->rhl", small_queries, small_keys_cache, preferred_element_type=jnp.float32
        )
        small_fresh_scores = jnp.einsum(
            "rhd,rhdn->rhn", small_queries, small_fresh_keys, preferred_element_type=jnp.float32
        )
        small_cached_weights, small_fresh_weights = attention_weights(
            small_cached_scores, small_fresh_scores, visible, HD
        )
        small_head_values = jnp.einsum(
            "rhl,rhdl->rhd",
            small_cached_weights,
            small_values_cache,
            preferred_element_type=jnp.float32,
        )
        small_head_values = small_head_values + jnp.einsum(
            "rhn,rhdn->rhd",
            small_fresh_weights,
            small_fresh_values,
            preferred_element_type=jnp.float32,
        )
        small_head_values = small_head_values.astype(jnp.bfloat16).reshape(
            row_count, small_heads * HD
        )
        small_partial = jnp.dot(
            small_head_values, small_output[0], preferred_element_type=jnp.float32
        )
        small_mixed = lax.psum(small_partial, "tp")
        small_hidden = small_full[step_index].astype(jnp.float32) + small_mixed
        small_final = norm_rows(small_hidden, small_final_gain[0])
        small_logits = lax.dot_general(
            small_final, small_table, (((1,), (1,)), ((), ())), preferred_element_type=jnp.float32
        )
        small_logits = small_logits.reshape(row_count, 2, small_table.shape[0] // 2)
        paired_logits = lax.all_to_all(
            small_logits[None], "grp", split_axis=2, concat_axis=0, tiled=True
        )
        normed = norm_rows(base_full[step_index], base_norm_gain)
        queries = jnp.dot(normed, base_query, preferred_element_type=jnp.float32).reshape(
            row_count, group_size, slice_width
        )
        queries = rotate_pairs(queries, positions, first_pair, HD).astype(jnp.bfloat16)
        new_key = jnp.dot(normed, base_keys_values[0], preferred_element_type=jnp.float32)
        key_now = rotate_pairs(new_key, positions, first_pair, HD).astype(jnp.bfloat16)
        value_now = jnp.dot(normed, base_keys_values[1], preferred_element_type=jnp.float32).astype(
            jnp.bfloat16
        )
        base_new_keys.append(key_now)
        base_new_values.append(value_now)
        fresh_keys = jnp.stack(base_new_keys, axis=-1)
        fresh_values = jnp.stack(base_new_values, axis=-1)
        cached_scores = jnp.einsum(
            "rgd,rdl->rgl", queries, base_keys_cache, preferred_element_type=jnp.float32
        )
        fresh_scores = jnp.einsum(
            "rgd,rdn->rgn", queries, fresh_keys, preferred_element_type=jnp.float32
        )
        both_scores = sum_slices(
            jnp.concatenate([cached_scores, fresh_scores], axis=-1), share_count
        )
        cached_weights, fresh_weights = attention_weights(
            both_scores[..., :CACHE], both_scores[..., CACHE:], visible, HD
        )
        head_values = jnp.einsum(
            "rgl,rdl->rgd", cached_weights, base_values_cache, preferred_element_type=jnp.float32
        )
        head_values = head_values + jnp.einsum(
            "rgn,rdn->rgd", fresh_weights, fresh_values, preferred_element_type=jnp.float32
        )
        head_values = head_values.astype(jnp.bfloat16).reshape(row_count, group_size * slice_width)
        partial_value = jnp.dot(head_values, base_output, preferred_element_type=jnp.float32)
        mixed_sum = lax.psum(partial_value, ("grp", "tp"))
        hidden = base_full[step_index].astype(jnp.float32) + mixed_sum
        final_rows = norm_rows(hidden, base_final_gain)
        base_logits = lax.dot_general(
            final_rows, base_unembed, (((1,), (1,)), ((), ())), preferred_element_type=jnp.float32
        )
        steered = base_logits + paired_logits[0, :, 0] - paired_logits[1, :, 0]
        local_max = jnp.max(steered, axis=-1)
        token_local = next_tokens[step_index] - block_index * vocab_width
        token_hit = jnp.arange(vocab_width)[None, :] == token_local[:, None]
        picked_local = jnp.sum(jnp.where(token_hit, steered, 0.0), axis=-1)
        row_max = lax.pmax(local_max, ("grp", "tp"))
        exp_total, picked = lax.psum(
            (jnp.sum(jnp.exp(steered - row_max[:, None]), axis=-1), picked_local), ("grp", "tp")
        )
        log_norm = row_max + jnp.log(exp_total)
        log_steps.append(steered - log_norm[:, None])
        chosen_total = chosen_total + picked - log_norm
    return (jnp.stack(log_steps, axis=0), chosen_total)


def solution(mesh):
    placed = (
        P(None, "dp", ("grp", "tp")),
        P("grp", None, "dp", "tp"),
        P(),
        P(None, ("grp", "tp")),
        P(None, None, ("grp", "tp")),
        P(("grp", "tp"), None),
        P(None, "dp", ("grp", "tp"), None),
        P(),
        P(("grp", "tp"), None),
        P("grp", None),
        P("grp", None, None, "tp"),
        P("grp", "tp", None),
        P("grp", None, "dp", "tp", None),
        P("grp", None),
        P("grp", None, "tp", None),
        P("dp"),
        P(None, "dp"),
    )
    return jax.shard_map(
        body,
        mesh=mesh,
        in_specs=placed,
        out_specs=(P(None, "dp", ("grp", "tp")), P("dp")),
        check_vma=False,
    )
```

profile of v0, /device:TPU:1, one launch (start us, length us, event | category | flops | bytes accessed | tf_op | source)
XLA Modules:
  0.0 1479.9 jit_solution(12581306323339910544)
XLA Ops:
  10.7 4.2 copy.267
  14.9 4.5 dot_general.205
  19.6 3.0 slice_bitcast_fusion
  29.4 89.5 %all-gather.6.cloned.1.call-done = bf16[1,3,64,4096]{3,2,1,0:T(8,128)(2,1)} async-done(((bf16[1,3,64,128]{3,2,1,0:T(8,128)(2,1)}), bf16[1,3,64,4096]{3,2,1,0:T(8,128)(2,1)}) %all-gather.6.cloned.1.call-update) | async-done | bytes 1572880 | tf_op jit(solution)/shard_map/all_gather | solution.py:96
  120.9 2.8 convolution_bitcast_fusion.4
  131.9 6.5 fusion
  153.3 95.0 %all-gather.4.cloned.1.call-done = bf16[3,64,8192]{2,1,0:T(8,128)(2,1)} async-done(((bf16[3,64,128]{2,1,0:T(8,128)(2,1)}), bf16[3,64,8192]{2,1,0:T(8,128)(2,1)}) %all-gather.4.cloned.1.call-update) | async-done | bytes 3145744 | tf_op jit(solution)/shard_map/all_gather | solution.py:95
  248.3 2.8 fusion.15
  264.8 3.3 fusion.34
  272.9 3.3 fusion.32
  283.8 11.9 collective-permute-done
  302.7 6.9 collective-permute-done.3
  314.3 3.7 collective-permute-start.4
  332.2 8.0 collective-permute-done.4
  348.2 6.0 collective-permute-done.7
  358.8 2.7 collective-permute-start.8
  370.0 6.9 collective-permute-done.8
  408.0 143.3 %all-reduce.9.cloned.1.call-done = (f32[64,4096]{1,0:T(8,128)}, f32[64,4096]{1,0:T(8,128)}, f32[64,4096]{1,0:T(8,128)}) async-done(((f32[64,4096]{1,0:T(8,128)}, f32[64,4096]{1,0:T(8,128)}, f32[64,4096]{1,0:T(8,128)}), (f32[64,4096]{1,0:T(8,128)}, f32[64,4096]{1,0:T(8,128)}, f32[64,4096]{1,0:T(8,128)})) %all-reduce.9.cloned.1.call-update) | async-done | bytes 3145744 | tf_op jit(solution)/shard_map/psum | solution.py:153
  551.3 3.0 multiply_reduce_fusion.5
  554.9 3.5 fusion.48
  558.4 25.1 %all-to-all-start = ((f32[1,64,2,256]{3,1,0,2:T(8,128)}), f32[1,64,2,256]{3,1,0,2:T(8,128)S(1)}, u32[]{:S(2)}, u32[]{:S(2)}) async-start(f32[1,64,2,256]{3,1,0,2:T(8,128)} %fusion.48), calls=%async_computation | async-start | bytes 262144 | tf_op jit(solution)/shard_map/all_to_all | solution.py:160
  583.6 4.6 fusion.51
  588.1 3.1 fusion.54
  591.2 574.1 %all-reduce.7.cloned.1.call-done = (f32[64,8192]{1,0:T(8,128)}, f32[64,8192]{1,0:T(8,128)}, f32[64,8192]{1,0:T(8,128)}) async-done(((f32[64,8192]{1,0:T(8,128)}, f32[64,8192]{1,0:T(8,128)}, f32[64,8192]{1,0:T(8,128)}), (f32[64,8192]{1,0:T(8,128)}, f32[64,8192]{1,0:T(8,128)}, f32[64,8192]{1,0:T(8,128)})) %all-reduce.7.cloned.1.call-update) | async-done | bytes 6291472 | tf_op jit(solution)/shard_map/psum | solution.py:197
  1165.4 4.8 multiply_reduce_fusion.2
  1170.2 3.4 all-to-all-start.1
  1173.6 4.7 fusion.290
  1178.3 3.7 all-to-all-start.2
  1182.0 4.7 fusion.289
  1186.7 4.7 fusion.288
  1191.3 140.0 %all-reduce.2 = (f32[64]{0:T(128)S(1)}, f32[64]{0:T(128)S(1)}, f32[64]{0:T(128)S(1)}) all-reduce(f32[64]{0:T(128)S(1)} %get-tuple-element.115, f32[64]{0:T(128)S(1)} %get-tuple-element.117, f32[64]{0:T(128)S(1)} %get-tuple-element.119), channel_id=1, replica_groups=mesh['grp'=2,'tp'=32,'dp'=2] {'grp','tp'}, use_global_device_ids=true, to_apply=%region_47.48 | all-reduce | flops 192 | bytes 1536 | tf_op jit(solution)/shard_map/pmax | solution.py:208
  1331.9 139.5 %all-reduce = (f32[64]{0:T(128)S(1)}, f32[64]{0:T(128)S(1)}, f32[64]{0:T(128)S(1)}, f32[64]{0:T(128)S(1)}, f32[64]{0:T(128)S(1)}, /*index=5*/f32[64]{0:T(128)S(1)}) all-reduce(f32[64]{0:T(128)S(1)} %get-tuple-element.22, f32[64]{0:T(128)S(1)} %get-tuple-element.20, ...), channel_id=1, replica_groups=mesh['grp'=2,'tp'=32,'dp'=2] {'grp','tp'}, use_global_device_ids=true, to_apply=%region_49.50 | all-reduce | flops 384 | bytes 3072 | tf_op jit(solution)/shard_map/psum | solution.py:209
  (320 shorter events, 141.5 us)
Async XLA Ops:
  7.2 394.7 %copy-start = (bf16[128,8192]{1,0:T(8,128)(2,1)S(1)}, bf16[128,8192]{1,0:T(8,128)(2,1)}, u32[]{:S(2)}) copy-start(bf16[128,8192]{1,0:T(8,128)(2,1)} %param.22) | copy-start | bytes 6291460
  7.2 111.7 %all-gather.6.cloned.1.call-start = ((), (), s32[]{:S(2)}) async-start(), calls=%async_computation.4 | async-start | bytes 1622016 | tf_op jit(solution)/shard_map/all_gather | solution.py:96
  7.9 240.4 %all-gather.4.cloned.1.call-start = ((), (), s32[]{:S(2)}) async-start(), calls=%async_computation.3 | async-start | bytes 3194880 | tf_op jit(solution)/shard_map/all_gather | solution.py:95
  8.7 542.6 %all-reduce.9.cloned.1.call-start = ((), (), s32[]{:S(2)}) async-start(), calls=%async_computation.6 | async-start | bytes 6291456 | tf_op jit(solution)/shard_map/psum | solution.py:153
  27.1 93.7 %copy-start.43 = (f32[1,4096]{1,0:T(1,128)S(1)}, f32[1,4096]{1,0:T(1,128)}, u32[]{:S(2)}) copy-start(f32[1,4096]{1,0:T(1,128)} %param.26) | copy-start | bytes 49156
  29.4 94.5 %copy-start.21 = (bf16[64,2,4096]{2,1,0:T(2,128)(2,1)S(1)}, bf16[64,2,4096]{2,1,0:T(2,128)(2,1)}, u32[]{:S(2)}) copy-start(bf16[64,2,4096]{2,1,0:T(2,128)(2,1)} %reshape.1691) | copy-start | bytes 3145732
  153.3 97.9 %copy-start.41 = (f32[8192]{0:T(1024)S(1)}, f32[8192]{0:T(1024)}, u32[]{:S(2)}) copy-start(f32[8192]{0:T(1024)} %param.19) | copy-start | bytes 98308
  153.3 1012.1 %all-reduce.7.cloned.1.call-start = ((), (), s32[]{:S(2)}) async-start(), calls=%async_computation.5 | async-start | bytes 12582912 | tf_op jit(solution)/shard_map/psum | solution.py:197
  264.1 53.9 %collective-permute-start.6 = (f32[64,8,131]{2,1,0:T(8,128)}, f32[64,8,131]{2,1,0:T(8,128)}, u32[]{:S(2)}, u32[]{:S(2)}) collective-permute-start(f32[64,8,131]{2,1,0:T(8,128)} %copy.330), channel_id=1, source_target_pairs={{0,2},{2,0},{4,6},{6,4},{8,10},{10,8},{12,14},{14,12},{16,18},{18,... | collective-permute-start | bytes 804872 | tf_op jit(solution)/shard_map/ppermute | solution.py:18
  271.9 23.8 %collective-permute-start = (f32[64,8,129]{2,1,0:T(8,128)}, f32[64,8,129]{2,1,0:T(8,128)}, u32[]{:S(2)}, u32[]{:S(2)}) collective-permute-start(f32[64,8,129]{2,1,0:T(8,128)} %copy.274), channel_id=1, source_target_pairs={{0,2},{2,0},{4,6},{6,4},{8,10},{10,8},{12,14},{14,12},{16,18},{18,... | collective-permute-start | bytes 792584 | tf_op jit(solution)/shard_map/ppermute | solution.py:18
  281.4 28.2 %collective-permute-start.3 = (f32[64,8,130]{2,1,0:T(8,128)}, f32[64,8,130]{2,1,0:T(8,128)}, u32[]{:S(2)}, u32[]{:S(2)}) collective-permute-start(f32[64,8,130]{2,1,0:T(8,128)} %copy.305), channel_id=1, source_target_pairs={{0,2},{2,0},{4,6},{6,4},{8,10},{10,8},{12,14},{14,12},{16,18},{18,... | collective-permute-start | bytes 798728 | tf_op jit(solution)/shard_map/ppermute | solution.py:18
  299.1 10.5 copy-start.12
  300.3 25.1 %collective-permute-start.1 = (f32[64,8,129]{2,1,0:T(8,128)}, f32[64,8,129]{2,1,0:T(8,128)}, u32[]{:S(2)}, u32[]{:S(2)}) collective-permute-start(f32[64,8,129]{2,1,0:T(8,128)} %copy.276), channel_id=1, source_target_pairs={{0,4},{2,6},{4,0},{6,2},{8,12},{10,14},{12,8},{14,10},{16,20},{18,... | collective-permute-start | bytes 792584 | tf_op jit(solution)/shard_map/ppermute | solution.py:18
  311.9 8.3 copy-start.28
  314.3 25.8 %collective-permute-start.4 = (f32[64,8,130]{2,1,0:T(8,128)}, f32[64,8,130]{2,1,0:T(8,128)}, u32[]{:S(2)}, u32[]{:S(2)}) collective-permute-start(f32[64,8,130]{2,1,0:T(8,128)} %copy.307), channel_id=1, source_target_pairs={{0,4},{2,6},{4,0},{6,2},{8,12},{10,14},{12,8},{14,10},{16,20},{18,... | collective-permute-start | bytes 798728 | tf_op jit(solution)/shard_map/ppermute | solution.py:18
  322.5 31.7 %collective-permute-start.7 = (f32[64,8,131]{2,1,0:T(8,128)}, f32[64,8,131]{2,1,0:T(8,128)}, u32[]{:S(2)}, u32[]{:S(2)}) collective-permute-start(f32[64,8,131]{2,1,0:T(8,128)} %copy.332), channel_id=1, source_target_pairs={{0,4},{2,6},{4,0},{6,2},{8,12},{10,14},{12,8},{14,10},{16,20},{18,... | collective-permute-start | bytes 804872 | tf_op jit(solution)/shard_map/ppermute | solution.py:18
  328.9 11.3 copy-start.11
  330.0 16.5 %copy-start.37 = (f32[64]{0:T(128)S(1)}, f32[64]{0:T(128)}, u32[]{:S(2)}) copy-start(f32[64]{0:T(128)} %copy-done.36) | copy-start | bytes 772
  330.0 32.3 %collective-permute-start.2 = (f32[64,8,129]{2,1,0:T(8,128)}, f32[64,8,129]{2,1,0:T(8,128)}, u32[]{:S(2)}, u32[]{:S(2)}) collective-permute-start(f32[64,8,129]{2,1,0:T(8,128)} %copy.278), channel_id=1, source_target_pairs={{0,8},{2,10},{4,12},{6,14},{8,0},{10,2},{12,4},{14,6},{16,24},{18,... | collective-permute-start | bytes 792584 | tf_op jit(solution)/shard_map/ppermute | solution.py:18
  343.6 10.6 copy-start.8
  344.8 21.9 %collective-permute-start.5 = (f32[64,8,130]{2,1,0:T(8,128)}, f32[64,8,130]{2,1,0:T(8,128)}, u32[]{:S(2)}, u32[]{:S(2)}) collective-permute-start(f32[64,8,130]{2,1,0:T(8,128)} %copy.309), channel_id=1, source_target_pairs={{0,8},{2,10},{4,12},{6,14},{8,0},{10,2},{12,4},{14,6},{16,24},{18,... | collective-permute-start | bytes 798728 | tf_op jit(solution)/shard_map/ppermute | solution.py:18
  357.5 9.1 copy-start.7
  358.8 10.1 copy-start.9
  358.8 18.1 %collective-permute-start.8 = (f32[64,8,131]{2,1,0:T(8,128)}, f32[64,8,131]{2,1,0:T(8,128)}, u32[]{:S(2)}, u32[]{:S(2)}) collective-permute-start(f32[64,8,131]{2,1,0:T(8,128)} %copy.334), channel_id=1, source_target_pairs={{0,8},{2,10},{4,12},{6,14},{8,0},{10,2},{12,4},{14,6},{16,24},{18,... | collective-permute-start | bytes 804872 | tf_op jit(solution)/shard_map/ppermute | solution.py:18
  368.9 11.5 copy-start.23
  388.2 9.1 copy-start.18
  388.2 12.5 copy-start.31
  554.9 28.6 %copy-start.16 = (f32[64,4096]{1,0:T(8,128)S(1)}, f32[64,4096]{1,0:T(8,128)}, u32[]{:S(2)}) copy-start(f32[64,4096]{1,0:T(8,128)} %get-tuple-element.48) | copy-start | bytes 3145732
  558.4 611.8 %all-to-all-start = ((f32[1,64,2,256]{3,1,0,2:T(8,128)}), f32[1,64,2,256]{3,1,0,2:T(8,128)S(1)}, u32[]{:S(2)}, u32[]{:S(2)}) async-start(f32[1,64,2,256]{3,1,0,2:T(8,128)} %fusion.48), calls=%async_computation | async-start | bytes 262144 | tf_op jit(solution)/shard_map/all_to_all | solution.py:160
  1165.4 8.2 copy-start.22
  1170.2 8.1 all-to-all-start.1
  1178.3 8.4 all-to-all-start.2
  (30 other events, 134.8 us)
Sparse Core Ops, SparseCore 0:
  9.6 109.2 all-gather.5
  120.5 127.7 all-gather.3
  251.0 300.2 all-reduce.8
  554.1 611.2 all-reduce.6
where the time goes:
time: 1490 us; the launch traced here: 1480 us
  waiting for transfers between devices  944 us (63%)
  blocking collectives  279 us (19%)
  matrix products  80.1 us (5%)
  local copies, waits for them, and re-layouts  65.8 us (4%)
  other arithmetic  47.6 us (3%)
  starting transfers between devices  47.2 us (3%)
  between operations  15.4 us (1%)
    psum x1, waiting for transfers between devices, body(): mixed_sum = lax.psum(partial_value, ('grp', 'tp'))  574 us
    psum x1, waiting for transfers between devices, body(): small_mixed = lax.psum(small_partial, 'tp')  143 us
    pmax x1, blocking collectives, body(): row_max = lax.pmax(local_max, ('grp', 'tp'))  140 us
    psum x1, blocking collectives, body(): lax.psum((jnp.sum(jnp.exp(steered - row_max[:, None]), axis=-1), picked_l...  139 us
    all_gather x1, waiting for transfers between devices, body(): base_full = lax.all_gather(base_inputs, ('grp', 'tp'), axis=2, tiled=True)  95 us
    all_gather x1, waiting for transfers between devices, body(): small_full = lax.all_gather(small_inputs[0], 'tp', axis=2, tiled=True)  89.5 us
    ppermute x9, waiting for transfers between devices, partner(): lax.ppermute(array, axis, [(i, i ^ 1 << bit) for i in range(lax.axis_size...  40.8 us
    all_to_all x3, starting transfers between devices, body(): lax.all_to_all(small_logits[None], 'grp', split_axis=2, concat_axis=0, ti...  32.2 us
  transfers between devices with their start and end apart: 16, of which 10 were waited for; matrix products, arithmetic and copies ran while one was open for 13% of the time, Pallas kernels for 0%

commit v1 on v0

v1 whole, which is shorter than its diff:
```python
import math

import jax
import jax.numpy as jnp
from jax import lax
from jax.sharding import Mesh, PartitionSpec as P

HD = 128
STEPS = 3
CACHE = 128
EPSILON = 1e-05
NEGATIVE = -1e30
CHIPS = ("z", "xl", "y")
EVERY = ("grp",) + CHIPS
PLANE = ("xl", "y")
F32 = jnp.float32
BF16 = jnp.bfloat16


def gather_chips(shard):
    count = lax.axis_size(CHIPS)
    copies = jnp.broadcast_to(shard[None], (count,) + shard.shape)
    return lax.all_to_all(copies, CHIPS, 0, 0, tiled=True)


def scatter_chips(blocks):
    received = lax.all_to_all(blocks, CHIPS, 0, 0, tiled=True)
    return jnp.sum(received.astype(F32), axis=0)


def swap_cores(array):
    return lax.ppermute(array, "grp", [(0, 1), (1, 0)])


def rotation(positions, first_pair, pair_count):
    pair_index = (first_pair + jnp.arange(pair_count)).astype(F32)
    frequency = jnp.exp(pair_index * (-2.0 * math.log(10000.0) / HD))
    angles = positions.astype(F32)[..., None] * frequency
    return jnp.cos(angles), jnp.sin(angles)


def rotate_pairs(values, cosine, sine):
    paired = values.reshape(values.shape[:-1] + (-1, 2))
    even, odd = paired[..., 0], paired[..., 1]
    turned = jnp.stack([even * cosine - odd * sine, even * sine + odd * cosine], axis=-1)
    return turned.reshape(values.shape)


def attend(queries, keys, values, fresh_keys, fresh_values, lengths):
    rows, steps, group, size = queries.shape
    factor = 1.0 / math.sqrt(HD)
    flat = queries.reshape(rows, steps * group, size)
    cached = jnp.einsum("rqd,rdl->rql", flat, keys, preferred_element_type=F32)
    fresh = jnp.einsum("rqd,rnd->rqn", flat, fresh_keys, preferred_element_type=F32)
    visible = (jnp.arange(CACHE)[None, :] < lengths[:, None])[:, None, :]
    step_of = jnp.arange(steps * group) // group
    seen = (jnp.arange(steps)[None, :] <= step_of[:, None])[None]
    cached = jnp.where(visible, cached * factor, NEGATIVE)
    fresh = jnp.where(seen, fresh * factor, NEGATIVE)
    top = jnp.maximum(jnp.max(cached, -1, keepdims=True), jnp.max(fresh, -1, keepdims=True))
    cached = jnp.exp(cached - top)
    fresh = jnp.exp(fresh - top)
    total = jnp.sum(cached, -1, keepdims=True) + jnp.sum(fresh, -1, keepdims=True)
    cached = (cached / total).astype(BF16)
    fresh = (fresh / total).astype(BF16)
    out = jnp.einsum("rql,rdl->rqd", cached, values, preferred_element_type=F32)
    out = out + jnp.einsum("rqn,rnd->rqd", fresh, fresh_values, preferred_element_type=F32)
    return out.astype(BF16).reshape(rows, steps, group, size)


def norm_rows(values, gain_row):
    values = values.astype(F32)
    scaling = lax.rsqrt(jnp.mean(values * values, axis=-1, keepdims=True) + EPSILON)
    return (values * scaling * gain_row).astype(BF16)


def body(
    base_inputs,
    small_inputs,
    base_norm_gain,
    base_query,
    base_keys_values,
    base_output,
    base_cache,
    base_final_gain,
    base_unembed,
    small_norm_gain,
    small_projections,
    small_output,
    small_cache,
    small_final_gain,
    small_unembed,
    lengths,
    next_tokens,
):
    rows = lengths.shape[0]
    every_row = STEPS * rows
    chips = lax.axis_size(CHIPS)
    shares = lax.axis_size(PLANE)
    core = lax.axis_index("grp")
    chip = lax.axis_index(CHIPS)
    block = core * chips + chip
    share = lax.axis_index(PLANE)
    width = base_inputs.shape[2]
    slice_width = base_keys_values.shape[2]
    group = base_query.shape[1] // slice_width
    part_rows = rows // shares
    vocab_width = base_unembed.shape[0]
    positions = lengths[None, :] + jnp.arange(STEPS)[:, None]

    def both_halves(mine):
        other = swap_cores(mine)
        return jnp.where(
            core == 0, jnp.concatenate([mine, other]), jnp.concatenate([other, mine])
        )

    def whole_rows(blocks):
        return blocks.transpose(1, 0, 2).reshape(every_row, -1)

    cache = base_cache.reshape(2, shares, part_rows, slice_width, CACHE).transpose(1, 0, 2, 3, 4)
    cache = lax.all_to_all(cache, PLANE, 0, 0, tiled=True)
    cache = cache.transpose(1, 2, 0, 3, 4).reshape(2, part_rows, HD, CACHE)

    base_in = base_inputs.reshape(every_row, width)
    small_in = small_inputs[0].reshape(every_row, width)
    inputs = gather_chips(jnp.stack([base_in, small_in]))
    base_full = whole_rows(both_halves(inputs[:, 0]))
    small_full = whole_rows(inputs[:, 1])

    base_normed = norm_rows(base_full, base_norm_gain)
    queries = jnp.dot(base_normed, base_query, preferred_element_type=F32)
    keys = jnp.dot(base_normed, base_keys_values[0], preferred_element_type=F32)
    values = jnp.dot(base_normed, base_keys_values[1], preferred_element_type=F32)
    cosine, sine = rotation(positions, share * (slice_width // 2), slice_width // 2)
    queries = rotate_pairs(
        queries.reshape(STEPS, rows, group, slice_width), cosine[:, :, None], sine[:, :, None]
    )
    keys = rotate_pairs(keys.reshape(STEPS, rows, slice_width), cosine, sine)
    packed = jnp.concatenate(
        [
            queries.reshape(STEPS, rows, group * slice_width),
            keys,
            values.reshape(STEPS, rows, slice_width),
        ],
        axis=-1,
    ).astype(BF16)
    packed = packed.reshape(STEPS, shares, part_rows, -1).transpose(1, 0, 2, 3)
    packed = lax.all_to_all(packed, PLANE, 0, 0, tiled=True)
    wide = group * slice_width
    queries = packed[..., :wide].reshape(shares, STEPS, part_rows, group, slice_width)
    queries = queries.transpose(2, 1, 3, 0, 4).reshape(part_rows, STEPS, group, HD)
    keys = packed[..., wide : wide + slice_width].transpose(2, 1, 0, 3)
    values = packed[..., wide + slice_width :].transpose(2, 1, 0, 3)
    part_lengths = lax.dynamic_slice_in_dim(lengths, share * part_rows, part_rows)
    heads = attend(
        queries,
        cache[0],
        cache[1],
        keys.reshape(part_rows, STEPS, HD),
        values.reshape(part_rows, STEPS, HD),
        part_lengths,
    )
    heads = heads.reshape(part_rows, STEPS, group, shares, slice_width).transpose(3, 1, 0, 2, 4)
    heads = lax.all_to_all(
        heads.reshape(shares, STEPS, part_rows, wide), PLANE, 0, 0, tiled=True
    )
    heads = heads.transpose(1, 0, 2, 3).reshape(every_row, wide)

    small_normed = norm_rows(small_full, small_norm_gain[0])
    cosine, sine = rotation(positions, 0, HD // 2)
    small_q, small_k, small_v = (
        jnp.dot(small_normed, small_projections[0, i], preferred_element_type=F32).reshape(
            STEPS, rows, HD
        )
        for i in range(3)
    )
    small_q = rotate_pairs(small_q, cosine, sine).astype(BF16).transpose(1, 0, 2)
    small_k = rotate_pairs(small_k, cosine, sine).astype(BF16).transpose(1, 0, 2)
    small_v = small_v.astype(BF16).transpose(1, 0, 2)
    small_heads = attend(
        small_q[:, :, None], small_cache[0, 0], small_cache[0, 1], small_k, small_v, lengths
    )
    small_heads = small_heads.transpose(1, 0, 2, 3).reshape(every_row, HD)

    def chip_blocks(array):
        return array.reshape(every_row, chips, width).transpose(1, 0, 2)

    base_mixed = jnp.dot(heads, base_output, preferred_element_type=F32)
    half = base_mixed.shape[1] // 2
    first, second = base_mixed[:, :half], base_mixed[:, half:]
    kept = jnp.where(core == 0, first, second)
    other = swap_cores(jnp.where(core == 0, second, first).astype(BF16))
    base_mixed = (kept + other.astype(F32)).astype(BF16)
    small_mixed = jnp.dot(small_heads, small_output[0], preferred_element_type=F32).astype(BF16)
    sums = scatter_chips(
        jnp.stack([chip_blocks(base_mixed), chip_blocks(small_mixed)], axis=1)
    )
    base_hidden = base_in.astype(F32) + sums[0]
    small_hidden = small_in.astype(F32) + sums[1]

    base_gain = lax.dynamic_slice_in_dim(base_final_gain, block * width, width)
    small_gain = lax.dynamic_slice_in_dim(small_final_gain[0], chip * width, width)
    finals = gather_chips(
        jnp.stack([base_hidden * base_gain, small_hidden * small_gain]).astype(BF16)
    )
    base_final = whole_rows(both_halves(finals[:, 0]))
    small_final = whole_rows(finals[:, 1])

    def row_scale(gained, gain):
        plain = gained.astype(F32) * (1.0 / gain)
        return lax.rsqrt(jnp.mean(plain * plain, axis=-1, keepdims=True) + EPSILON)

    across = (((1,), (1,)), ((), ()))
    base_logits = lax.dot_general(base_final, base_unembed, across, preferred_element_type=F32)
    base_logits = base_logits * row_scale(base_final, base_final_gain)
    table = small_unembed[0].reshape(-1, small_unembed.shape[3])
    small_logits = lax.dot_general(small_final, table, across, preferred_element_type=F32)
    small_logits = small_logits * row_scale(small_final, small_final_gain[0])
    low, high = small_logits[:, :vocab_width], small_logits[:, vocab_width:]
    theirs = swap_cores(jnp.where(core == 0, high, low))
    ours = jnp.where(core == 0, low, high)
    steered = base_logits + jnp.where(core == 0, ours - theirs, theirs - ours)

    local_max = jnp.max(steered, axis=-1)
    local_sum = jnp.sum(jnp.exp(steered - local_max[:, None]), axis=-1)
    local_token = next_tokens.reshape(every_row) - block * vocab_width
    hit = jnp.arange(vocab_width)[None, :] == local_token[:, None]
    picked = jnp.sum(jnp.where(hit, steered, 0.0), axis=-1)
    triple = jnp.stack([local_max, local_sum, picked])
    count = lax.axis_size(EVERY)
    triples = lax.all_to_all(
        jnp.broadcast_to(triple[None], (count,) + triple.shape), EVERY, 0, 0, tiled=True
    )
    top = jnp.max(triples[:, 0], axis=0)
    total = jnp.sum(triples[:, 1] * jnp.exp(triples[:, 0] - top[None]), axis=0)
    log_norm = top + jnp.log(total)
    chosen = jnp.sum(triples[:, 2], axis=0) - log_norm
    log_probs = (steered - log_norm[:, None]).reshape(STEPS, rows, vocab_width)
    return log_probs, jnp.sum(chosen.reshape(STEPS, rows), axis=0)


def solution(mesh):
    devices = mesh.devices
    fine = Mesh(devices.reshape(2, 4, 2, 4, 2), ("grp", "z", "xl", "y", "dp"))
    placed = (
        P(None, "dp", EVERY),
        P("grp", None, "dp", CHIPS),
        P(),
        P(None, EVERY),
        P(None, None, EVERY),
        P(EVERY, None),
        P(None, "dp", EVERY, None),
        P(),
        P(EVERY, None),
        P("grp", None),
        P("grp", None, None, CHIPS),
        P("grp", CHIPS, None),
        P("grp", None, "dp", CHIPS, None),
        P("grp", None),
        P("grp", None, CHIPS, None),
        P("dp"),
        P(None, "dp"),
    )
    return jax.shard_map(
        body,
        mesh=fine,
        in_specs=placed,
        out_specs=(P(None, "dp", EVERY), P("dp")),
        check_vma=False,
    )
```

time: 1490 us -> 321 us (0.22)
  waiting for transfers between devices: 944 us -> 110 us
  blocking collectives: 279 us -> 15.3 us
  matrix products: 80.1 us -> 34.8 us
  other arithmetic: 47.6 us -> 31.3 us
    psum x2 -> x0, waiting for transfers between devices: 717 us -> none  [the longest x1 574 us: body(): mixed_sum = lax.psum(partial_value, ('grp', 'tp'))]
    all_gather x2 -> x0, waiting for transfers between devices: 185 us -> none  [the longest x1 95 us: body(): base_full = lax.all_gather(base_inputs, ('grp', 'tp'), axis=2, tiled=True)]
    pmax x1 -> x0, blocking collectives: 140 us -> none  [body(): row_max = lax.pmax(local_max, ('grp', 'tp'))]
    psum x1 -> x0, blocking collectives: 139 us -> none  [body(): lax.psum((jnp.sum(jnp.exp(steered - row_max[:, None]), axis=-1), picked_l...]
    all_to_all x3 -> x6, waiting for transfers between devices: 0.01 us -> 110 us  [the longest x2 64.2 us: gather_chips(): return lax.all_to_all(copies, CHIPS, 0, 0, tiled=True)]
    dot_general x45 -> x18, matrix products: 80.1 us -> 34.8 us  [the longest x3 7.02 us: body(): jnp.dot(small_normed, small_projections[0, i], preferred_element_type=F32)]
    ppermute x9 -> x4, waiting for transfers between devices: 40.8 us -> 0.01 us  [swap_cores(): return lax.ppermute(array, 'grp', [(0, 1), (1, 0)])]
    convert_element_type x18 -> x10, local copies, waits for them, and re-layouts: 8.61 us -> 32.6 us  [the longest x7 31 us: norm_rows(): return (values * scaling * gain_row).astype(BF16)]
  transfers between devices with their start and end apart: 16 -> 10, of which waited for: 10 -> 5; matrix products, arithmetic and copies ran while one was open for 13% -> 20% of each run, Pallas kernels for 0% -> 0%
where the time goes in v1:
time: 321 us; the launch traced here: 316 us
  waiting for transfers between devices  110 us (34%)
  local copies, waits for them, and re-layouts  72.6 us (23%)
  starting transfers between devices  49.6 us (15%)
  matrix products  34.8 us (11%)
  other arithmetic  31.3 us (10%)
  blocking collectives  15.3 us (5%)
    all_to_all x2, waiting for transfers between devices, gather_chips(): return lax.all_to_all(copies, CHIPS, 0, 0, tiled=True)  64.2 us
    all_to_all x1, waiting for transfers between devices, scatter_chips(): received = lax.all_to_all(blocks, CHIPS, 0, 0, tiled=True)  40.4 us
    convert_element_type x7, local copies, waits for them, and re-layouts, norm_rows(): return (values * scaling * gain_row).astype(BF16)  31 us
    all_to_all x2, starting transfers between devices, gather_chips(): return lax.all_to_all(copies, CHIPS, 0, 0, tiled=True)  17.2 us
    all_to_all x1, blocking collectives, body(): lax.all_to_all(jnp.broadcast_to(triple[None], (count,) + triple.shape), E...  15.3 us
    ppermute x4, starting transfers between devices, swap_cores(): return lax.ppermute(array, 'grp', [(0, 1), (1, 0)])  13.1 us
    dot_general x5, local copies, waits for them, and re-layouts, body(): jnp.dot(small_normed, small_projections[0, i], preferred_element_type=F32)  8.98 us
    dot_general x2, local copies, waits for them, and re-layouts, body(): queries = jnp.dot(base_normed, base_query, preferred_element_type=F32)  8.51 us
  transfers between devices with their start and end apart: 10, of which 5 were waited for; matrix products, arithmetic and copies ran while one was open for 20% of the time, Pallas kernels for 0%

profile of v1, /device:TPU:1, one launch (start us, length us, event | category | flops | bytes accessed | tf_op | source)
XLA Modules:
  0.0 315.5 jit_solution(5268859101294959551)
XLA Ops:
  2.7 5.9 %all-to-all-start.2 = ((bf16[8,2,8,16,128]{4,3,2,1,0:T(8,128)(2,1)}), bf16[8,2,8,16,128]{4,3,2,1,0:T(8,128)(2,1)}, u32[]{:S(2)}, u32[]{:S(2)}) async-start(bf16[8,2,8,16,128]{4,3,2,1,0:T(8,128)(2,1)} %copy.286), calls=%async_computation.2 | async-start | bytes 1048576 | tf_op jit(solution)/shard_map/all_to_all | solution.py:121
  8.6 3.0 slice_bitcast_fusion.4
  20.1 9.3 %all-to-all-start = ((bf16[32,2,192,128]{3,2,1,0:T(8,128)(2,1)}), bf16[32,2,192,128]{3,2,1,0:T(8,128)(2,1)}, u32[]{:S(2)}, u32[]{:S(2)}) async-start(bf16[32,2,192,128]{3,2,1,0:T(8,128)(2,1)} %broadcast_in_dim.50), calls=%async_computation | async-start | bytes 6291456 | tf_op jit(solution)/shard_map/all_to_all | solution.py:23
  30.3 4.1 %copy.277 = bf16[128,8192]{1,0:T(8,128)(2,1)} copy(bf16[128,8192]{0,1:T(8,128)(2,1)} %bitcast.222) | data formatting | bytes 4194304 | tf_op jit(solution)/shard_map/dot_general | solution.py:131
  34.4 4.4 %dot_general.71 = bf16[8,8,2,8192]{3,2,1,0:T(2,128)(2,1)} reshape(bf16[128,8192]{1,0:T(8,128)(2,1)} %copy.277) | data formatting | bytes 4194304 | tf_op jit(solution)/shard_map/dot_general | solution.py:131
  44.4 23.5 %all-to-all-done = bf16[32,2,192,128]{3,2,1,0:T(8,128)(2,1)} async-done(((bf16[32,2,192,128]{3,2,1,0:T(8,128)(2,1)}), bf16[32,2,192,128]{3,2,1,0:T(8,128)(2,1)}, u32[]{:S(2)}, u32[]{:S(2)}) %all-to-all-start) | async-done | bytes 3145760 | tf_op jit(solution)/shard_map/all_to_all | solution.py:23
  70.6 6.6 %collective-permute-start = (bf16[32,192,128]{2,1,0:T(8,128)(2,1)}, bf16[32,192,128]{2,1,0:T(8,128)(2,1)}, u32[]{:S(2)}, u32[]{:S(2)}) collective-permute-start(bf16[32,192,128]{2,1,0:T(8,128)(2,1)} %slice_bitcast_fusion.2), channel_id=1, source_target_pairs={{0,64},{64,0},{1,65},{65,1},{2,66},{66,2},{3,67},{67,3},{4,68},{68... | collective-permute-start | bytes 4718600 | tf_op jit(solution)/shard_map/ppermute | solution.py:32
  83.2 3.7 %reshape.502 = bf16[3,64,4096,1]{2,1,0,3:T(8,128)(2,1)} reshape(bf16[192,32,128]{2,1,0:T(8,128)(2,1)} %copy.296) | data formatting | bytes 3145728 | tf_op jit(solution)/shard_map/convert_element_type | solution.py:74
  86.9 3.1 fusion.27
  93.9 4.6 %fusion = f32[192]{0:T(256)S(1)} fusion(bf16[32,192,128]{2,1,0:T(8,128)(2,1)} %slice_bitcast_fusion.2, bf16[32,192,128]{2,1,0:T(8,128)(2,1)} %collective-permute-done, pred[]{:T(512)S(6)} %eq.8), kind=kLoop, calls=%fused_computation.2 | loop fusion | flops 9436992 | bytes 3146497 | tf_op jit(solution)/shard_map/reduce_sum | solution.py:73
  98.4 3.7 %fusion.6 = bf16[192,64,128]{2,0,1:T(8,128)(2,1)S(1)} fusion(f32[64,128]{1,0:T(8,128)S(1)} %bitcast.238, f32[192]{0:T(256)S(1)} %add_rsqrt_fusion.3, bf16[32,192,128]{2,1,0:T(8,128)(2,1)} %slice_bitcast_fusion.2, bf16[32,192,128]{2,1,0:T(8,128)(2,1)} %collective-permute-done, pred[]{:T(512)S(6)} %eq.8), kind=kLoop, calls=%fused_computation.13 | loop fusion | flops 11010048 | bytes 6324993 | tf_op jit(solution)/shard_map/convert_element_type | solution.py:74
  102.1 3.7 %copy.276 = bf16[192,64,128]{2,1,0:T(8,128)(2,1)} copy(bf16[192,64,128]{2,0,1:T(8,128)(2,1)S(1)} %fusion.6) | data formatting | bytes 6291456 | tf_op jit(solution)/shard_map/convert_element_type | solution.py:74
  105.9 5.8 %convert_element_type.193 = bf16[3,8,8,8192]{3,2,1,0:T(8,128)(2,1)} reshape(bf16[192,64,128]{2,1,0:T(8,128)(2,1)} %copy.276) | data formatting | bytes 6291456 | tf_op jit(solution)/shard_map/convert_element_type | solution.py:74
  111.7 5.8 %reshape.499 = bf16[3,64,8192,1]{2,1,0,3:T(8,128)(2,1)} reshape(bf16[192,64,128]{2,1,0:T(8,128)(2,1)} %copy.276) | data formatting | bytes 6291456 | tf_op jit(solution)/shard_map/convert_element_type | solution.py:74
  117.5 6.1 %reshape.497 = bf16[3,64,8192,1,1]{2,1,0,3,4:T(8,128)(2,1)} reshape(bf16[192,64,128]{2,1,0:T(8,128)(2,1)} %copy.276) | data formatting | bytes 6291456 | tf_op jit(solution)/shard_map/convert_element_type | solution.py:74
  123.6 2.9 convolution_convert_fusion.1
  126.6 3.1 fusion.10
  130.6 4.3 %fusion.12 = f32[3,64,8,8,2]{1,3,4,2,0:T(8,128)S(1)} fusion(bf16[3,64,8192,1,1]{2,1,0,3,4:T(8,128)(2,1)} %reshape.497, bf16[8,8,2,8192]{3,2,1,0:T(2,128)(2,1)} %dot_general.71), kind=kOutput, calls=%fused_computation.22 | convolution fusion | flops 402653184 | bytes 5341184 | tf_op jit(solution)/shard_map/dot_general | solution.py:131
  139.2 3.5 %all-to-all-start.1 = ((bf16[8,3,8,160]{3,2,1,0:T(8,128)(2,1)}), bf16[8,3,8,160]{3,2,1,0:T(8,128)(2,1)S(1)}, u32[]{:S(2)}, u32[]{:S(2)}) async-start(bf16[8,3,8,160]{3,2,1,0:T(8,128)(2,1)} %copy.284), calls=%async_computation.1 | async-start | bytes 196608 | tf_op jit(solution)/shard_map/all_to_all | solution.py:148
  143.9 4.1 %all-to-all-done.1 = bf16[8,3,8,160]{3,2,1,0:T(8,128)(2,1)S(1)} async-done(((bf16[8,3,8,160]{3,2,1,0:T(8,128)(2,1)}), bf16[8,3,8,160]{3,2,1,0:T(8,128)(2,1)S(1)}, u32[]{:S(2)}, u32[]{:S(2)}) %all-to-all-start.1) | async-done | bytes 61472 | tf_op jit(solution)/shard_map/all_to_all | solution.py:148
  152.6 3.3 %all-to-all-start.3 = ((bf16[8,3,8,128]{3,2,1,0:T(8,128)(2,1)}), bf16[8,3,8,128]{3,2,1,0:T(8,128)(2,1)S(1)}, u32[]{:S(2)}, u32[]{:S(2)}) async-start(bf16[8,3,8,128]{3,2,1,0:T(8,128)(2,1)} %reshape.487), calls=%async_computation.3 | async-start | bytes 98304 | tf_op jit(solution)/shard_map/all_to_all | solution.py:164
  156.1 3.7 %convert_element_type.204 = bf16[3,64,4096]{2,1,0:T(8,128)(2,1)} reshape(bf16[192,32,128]{2,1,0:T(8,128)(2,1)} %copy.296) | data formatting | bytes 3145728 | tf_op jit(solution)/shard_map/convert_element_type | solution.py:74
  168.7 3.0 fusion.14
  179.2 6.5 %all-to-all-start.4 = ((bf16[32,2,192,128]{3,2,1,0:T(8,128)(2,1)}), bf16[32,2,192,128]{3,2,1,0:T(8,128)(2,1)S(1)}, u32[]{:S(2)}, u32[]{:S(2)}) async-start(bf16[32,2,192,128]{3,2,1,0:T(8,128)(2,1)} %pad_maximum_fusion), calls=%async_computation.4 | async-start | bytes 6291456 | tf_op jit(solution)/shard_map/all_to_all | solution.py:27
  185.9 40.4 %all-to-all-done.4 = bf16[32,2,192,128]{3,2,1,0:T(8,128)(2,1)S(1)} async-done(((bf16[32,2,192,128]{3,2,1,0:T(8,128)(2,1)}), bf16[32,2,192,128]{3,2,1,0:T(8,128)(2,1)S(1)}, u32[]{:S(2)}, u32[]{:S(2)}) %all-to-all-start.4) | async-done | bytes 3145760 | tf_op jit(solution)/shard_map/all_to_all | solution.py:27
  229.2 7.9 %all-to-all-start.5 = ((bf16[32,2,192,128]{3,2,1,0:T(8,128)(2,1)}), bf16[32,2,192,128]{3,2,1,0:T(8,128)(2,1)S(1)}, u32[]{:S(2)}, u32[]{:S(2)}) async-start(bf16[32,2,192,128]{3,2,1,0:T(8,128)(2,1)} %broadcast_in_dim.66), calls=%async_computation.5 | async-start | bytes 6291456 | tf_op jit(solution)/shard_map/all_to_all | solution.py:23
  237.2 40.6 %all-to-all-done.5 = bf16[32,2,192,128]{3,2,1,0:T(8,128)(2,1)S(1)} async-done(((bf16[32,2,192,128]{3,2,1,0:T(8,128)(2,1)}), bf16[32,2,192,128]{3,2,1,0:T(8,128)(2,1)S(1)}, u32[]{:S(2)}, u32[]{:S(2)}) %all-to-all-start.5) | async-done | bytes 3145760 | tf_op jit(solution)/shard_map/all_to_all | solution.py:23
  279.7 3.6 %collective-permute-start.2 = (bf16[32,192,128]{2,1,0:T(8,128)(2,1)}, bf16[32,192,128]{2,1,0:T(8,128)(2,1)}, u32[]{:S(2)}, u32[]{:S(2)}) collective-permute-start(bf16[32,192,128]{2,1,0:T(8,128)(2,1)} %get-tuple-element.9), channel_id=1, source_target_pairs={{0,64},{64,0},{1,65},{65,1},{2,66},{66,2},{3,67},{67,3},{4,68},{68... | collective-permute-start | bytes 4718600 | tf_op jit(solution)/shard_map/ppermute | solution.py:32
  284.0 4.3 %fusion.32 = f32[192,512]{1,0:T(8,128)S(1)} fusion(bf16[512,4096]{1,0:T(8,128)(2,1)} %bitcast.243, bf16[32,24,8,128]{3,2,1,0:T(8,128)(2,1)} %get-tuple-element.8, f32[192]{0:T(256)S(1)} %add_rsqrt_fusion), kind=kOutput, calls=%fused_computation.51 | convolution fusion | flops 805404672 | bytes 6161152 | tf_op jit(solution)/shard_map/dot_general | solution.py:217
  288.4 4.6 %multiply_reduce_fusion = f32[192]{0:T(256)S(1)} fusion(f32[64,128]{1,0:T(8,128)S(1)} %divide_bitcast_fusion, bf16[32,192,128]{2,1,0:T(8,128)(2,1)} %get-tuple-element.9, bf16[32,192,128]{2,1,0:T(8,128)(2,1)} %collective-permute-done.2, pred[]{:T(512)S(6)} %eq.8), kind=kLoop, calls=%fused_computation.5 | loop fusion | flops 11009856 | bytes 3179265 | tf_op jit(solution)/shard_map/reduce_sum | solution.py:211
  293.1 4.7 %fusion.119 = (f32[192]{0:T(256)S(1)}, f32[192,256]{1,0:T(8,128)S(1)}) fusion(f32[192,256]{1,0:T(8,128)S(1)} %collective-permute-done.3, f32[192,512]{1,0:T(8,128)S(1)} %fusion.32, pred[]{:T(512)S(6)} %eq.8, f32[192]{0:T(256)S(1)} %add_rsqrt_fusion.1, bf16[256,8192]{1,0:T(8,128)(2,1)S(1)} %copy-done.33, bf16[32,192,128]{2,1,0:T(8,128)(2,1)} %get-tuple-element.9, ...), kind=kOutput, calls=%fused_computation.195 | convolution fusion | flops 810368832 | bytes 8129024 | tf_op jit(solution)/shard_map/dot_general | solution.py:214
  298.1 15.3 %all_to_all.35 = f32[64,3,192]{2,1,0:T(4,128)S(1)} all-to-all(f32[64,3,192]{2,1,0:T(4,128)S(1)} %broadcast_in_dim.68), channel_id=1, replica_groups=mesh['grp'=2,'z'=4,'xl'=2,'y'=4,'dp'=2] {'grp','z','xl','y'}, dimensions={0} | all-to-all | bytes 294912 | tf_op jit(solution)/shard_map/all_to_all | solution.py:231
  (197 shorter events, 64.4 us)
Async XLA Ops:
  0.6 160.4 %copy-start = (bf16[128,8192]{1,0:T(8,128)(2,1)S(1)}, bf16[128,8192]{1,0:T(8,128)(2,1)}, u32[]{:S(2)}) copy-start(bf16[128,8192]{1,0:T(8,128)(2,1)} %param.22) | copy-start | bytes 6291460
  2.7 15.0 %all-to-all-start.2 = ((bf16[8,2,8,16,128]{4,3,2,1,0:T(8,128)(2,1)}), bf16[8,2,8,16,128]{4,3,2,1,0:T(8,128)(2,1)}, u32[]{:S(2)}, u32[]{:S(2)}) async-start(bf16[8,2,8,16,128]{4,3,2,1,0:T(8,128)(2,1)} %copy.286), calls=%async_computation.2 | async-start | bytes 1048576 | tf_op jit(solution)/shard_map/all_to_all | solution.py:121
  20.1 9.3 %copy-start.8 = (bf16[2,8192,16]{1,2,0:T(8,128)(2,1)S(1)}, bf16[2,8192,16]{1,2,0:T(8,128)(2,1)}, u32[]{:S(2)}) copy-start(bf16[2,8192,16]{1,2,0:T(8,128)(2,1)} %param.21) | copy-start | bytes 1572868
  20.1 47.8 %all-to-all-start = ((bf16[32,2,192,128]{3,2,1,0:T(8,128)(2,1)}), bf16[32,2,192,128]{3,2,1,0:T(8,128)(2,1)}, u32[]{:S(2)}, u32[]{:S(2)}) async-start(bf16[32,2,192,128]{3,2,1,0:T(8,128)(2,1)} %broadcast_in_dim.50), calls=%async_computation | async-start | bytes 6291456 | tf_op jit(solution)/shard_map/all_to_all | solution.py:23
  43.6 35.3 %copy-start.21 = (f32[1,4096]{1,0:T(1,128)S(1)}, f32[1,4096]{1,0:T(1,128)}, u32[]{:S(2)}) copy-start(f32[1,4096]{1,0:T(1,128)} %param.26) | copy-start | bytes 49156
  70.6 23.2 %collective-permute-start = (bf16[32,192,128]{2,1,0:T(8,128)(2,1)}, bf16[32,192,128]{2,1,0:T(8,128)(2,1)}, u32[]{:S(2)}, u32[]{:S(2)}) collective-permute-start(bf16[32,192,128]{2,1,0:T(8,128)(2,1)} %slice_bitcast_fusion.2), channel_id=1, source_target_pairs={{0,64},{64,0},{1,65},{65,1},{2,66},{66,2},{3,67},{67,3},{4,68},{68... | collective-permute-start | bytes 4718600 | tf_op jit(solution)/shard_map/ppermute | solution.py:32
  81.0 5.9 %copy-start.4 = (bf16[64,2,4096]{2,1,0:T(2,128)(2,1)S(1)}, bf16[64,2,4096]{2,1,0:T(2,128)(2,1)}, u32[]{:S(2)}) copy-start(bf16[64,2,4096]{2,1,0:T(2,128)(2,1)} %dot_general.87) | copy-start | bytes 3145732
  91.6 6.8 %copy-start.16 = (f32[8192]{0:T(1024)S(1)}, f32[8192]{0:T(1024)}, u32[]{:S(2)}) copy-start(f32[8192]{0:T(1024)} %param.19) | copy-start | bytes 98308
  117.4 6.1 %copy-start.9 = (bf16[2,8192,16]{1,2,0:T(8,128)(2,1)S(1)}, bf16[2,8192,16]{1,2,0:T(8,128)(2,1)}, u32[]{:S(2)}) copy-start(bf16[2,8192,16]{1,2,0:T(8,128)(2,1)} %param.21) | copy-start | bytes 1572868
  123.5 6.1 %copy-start.19 = (f32[3,64]{1,0:T(4,128)S(1)}, f32[3,64]{1,0:T(4,128)}, u32[]{:S(2)}) copy-start(f32[3,64]{1,0:T(4,128)} %copy-done.17) | copy-start | bytes 2308
  123.5 6.1 %copy-start.27 = (f32[8]{0:T(128)S(1)}, f32[8]{0:T(128)}, u32[]{:S(2)}) copy-start(f32[8]{0:T(128)} %copy-done.26) | copy-start | bytes 100
  135.1 13.9 %copy-start.30 = (pred[8,128]{1,0:T(8,128)(4,1)S(1)}, pred[8,128]{1,0:T(8,128)(4,1)}, u32[]{:S(2)}) copy-start(pred[8,128]{1,0:T(8,128)(4,1)} %iota_compare_fusion.2) | copy-start | bytes 3076
  136.5 12.8 %copy-start.34 = (pred[24,3]{0,1:T(4,128)(4,1)S(1)}, pred[24,3]{0,1:T(4,128)(4,1)}, u32[]{:S(2)}) copy-start(pred[24,3]{0,1:T(4,128)(4,1)} %iota_compare_fusion.4) | copy-start | bytes 220
  139.2 16.7 %copy-start.24 = (pred[3,3]{1,0:T(4,128)(4,1)S(1)}, pred[3,3]{1,0:T(4,128)(4,1)}, u32[]{:S(2)}) copy-start(pred[3,3]{1,0:T(4,128)(4,1)} %iota_compare_fusion.3) | copy-start | bytes 31
  139.2 8.8 %all-to-all-start.1 = ((bf16[8,3,8,160]{3,2,1,0:T(8,128)(2,1)}), bf16[8,3,8,160]{3,2,1,0:T(8,128)(2,1)S(1)}, u32[]{:S(2)}, u32[]{:S(2)}) async-start(bf16[8,3,8,160]{3,2,1,0:T(8,128)(2,1)} %copy.284), calls=%async_computation.1 | async-start | bytes 196608 | tf_op jit(solution)/shard_map/all_to_all | solution.py:148
  152.6 8.4 %all-to-all-start.3 = ((bf16[8,3,8,128]{3,2,1,0:T(8,128)(2,1)}), bf16[8,3,8,128]{3,2,1,0:T(8,128)(2,1)S(1)}, u32[]{:S(2)}, u32[]{:S(2)}) async-start(bf16[8,3,8,128]{3,2,1,0:T(8,128)(2,1)} %reshape.487), calls=%async_computation.3 | async-start | bytes 98304 | tf_op jit(solution)/shard_map/all_to_all | solution.py:164
  162.0 5.8 %copy-start.2 = (f32[192,8192]{1,0:T(8,128)}, f32[192,8192]{1,0:T(8,128)S(1)}, u32[]{:S(2)}) copy-start(f32[192,8192]{1,0:T(8,128)S(1)} %fusion.120) | copy-start | bytes 18874372
  162.1 5.0 %copy-start.32 = (bf16[1,2,64,128,128]{4,3,2,1,0:T(8,128)(2,1)S(1)}, bf16[1,2,64,128,128]{4,3,2,1,0:T(8,128)(2,1)}, u32[]{:S(2)}) copy-start(bf16[1,2,64,128,128]{4,3,2,1,0:T(8,128)(2,1)} %param.29) | copy-start | bytes 12582916
  162.1 5.8 %copy-start.25 = (pred[3,3]{1,0:T(4,128)(4,1)S(1)}, pred[3,3]{1,0:T(4,128)(4,1)}, u32[]{:S(2)}) copy-start(pred[3,3]{1,0:T(4,128)(4,1)} %iota_compare_fusion.3) | copy-start | bytes 31
  163.5 11.9 %collective-permute-start.1 = (bf16[192,4096]{1,0:T(8,128)(2,1)}, bf16[192,4096]{1,0:T(8,128)(2,1)}, u32[]{:S(2)}, u32[]{:S(2)}) collective-permute-start(bf16[192,4096]{1,0:T(8,128)(2,1)} %select_convert_fusion), channel_id=1, source_target_pairs={{0,64},{64,0},{1,65},{65,1},{2,66},{66,2},{3,67},{67,3},{4,68},{68... | collective-permute-start | bytes 4718600 | tf_op jit(solution)/shard_map/ppermute | solution.py:32
  168.3 7.0 %slice-start = ((s8[6291456]{0:T(1024)(128)(4,1)}), s8[2097152]{0:T(1024)(128)(4,1)S(1)}, s32[]{:S(2)}) async-start(s8[6291456]{0:T(1024)(128)(4,1)} %bitcast.219), calls=%async_computation.7 | async-start | bytes 4194304
  168.7 5.7 %copy-start.6 = (bf16[1,128,4096]{2,1,0:T(8,128)(2,1)S(1)}, bf16[1,128,4096]{2,1,0:T(8,128)(2,1)}, u32[]{:S(2)}) copy-start(bf16[1,128,4096]{2,1,0:T(8,128)(2,1)} %param.28) | copy-start | bytes 3145732
  179.2 6.6 %copy-start.20 = (f32[8192]{0:T(1024)S(1)}, f32[8192]{0:T(1024)}, u32[]{:S(2)}) copy-start(f32[8192]{0:T(1024)} %param.24) | copy-start | bytes 98308
  179.2 6.7 %copy-start.22 = (f32[1,4096]{1,0:T(1,128)S(1)}, f32[1,4096]{1,0:T(1,128)}, u32[]{:S(2)}) copy-start(f32[1,4096]{1,0:T(1,128)} %param.30) | copy-start | bytes 49156
  179.2 47.1 %all-to-all-start.4 = ((bf16[32,2,192,128]{3,2,1,0:T(8,128)(2,1)}), bf16[32,2,192,128]{3,2,1,0:T(8,128)(2,1)S(1)}, u32[]{:S(2)}, u32[]{:S(2)}) async-start(bf16[32,2,192,128]{3,2,1,0:T(8,128)(2,1)} %pad_maximum_fusion), calls=%async_computation.4 | async-start | bytes 6291456 | tf_op jit(solution)/shard_map/all_to_all | solution.py:27
  185.8 41.0 %copy-start.13 = (bf16[3,64,128]{2,1,0:T(8,128)(2,1)S(1)}, bf16[3,64,128]{2,1,0:T(8,128)(2,1)}, u32[]{:S(2)}) copy-start(bf16[3,64,128]{2,1,0:T(8,128)(2,1)} %param.17) | copy-start | bytes 147460
  229.2 48.6 %all-to-all-start.5 = ((bf16[32,2,192,128]{3,2,1,0:T(8,128)(2,1)}), bf16[32,2,192,128]{3,2,1,0:T(8,128)(2,1)S(1)}, u32[]{:S(2)}, u32[]{:S(2)}) async-start(bf16[32,2,192,128]{3,2,1,0:T(8,128)(2,1)} %broadcast_in_dim.66), calls=%async_computation.5 | async-start | bytes 6291456 | tf_op jit(solution)/shard_map/all_to_all | solution.py:23
  237.2 46.2 %copy-start.29 = (s32[3,64]{1,0:T(4,128)S(1)}, s32[3,64]{1,0:T(4,128)}, u32[]{:S(2)}) copy-start(s32[3,64]{1,0:T(4,128)} %param.33) | copy-start | bytes 2308
  279.7 8.7 %collective-permute-start.2 = (bf16[32,192,128]{2,1,0:T(8,128)(2,1)}, bf16[32,192,128]{2,1,0:T(8,128)(2,1)}, u32[]{:S(2)}, u32[]{:S(2)}) collective-permute-start(bf16[32,192,128]{2,1,0:T(8,128)(2,1)} %get-tuple-element.9), channel_id=1, source_target_pairs={{0,64},{64,0},{1,65},{65,1},{2,66},{66,2},{3,67},{67,3},{4,68},{68... | collective-permute-start | bytes 4718600 | tf_op jit(solution)/shard_map/ppermute | solution.py:32
  284.0 9.1 %copy-start.33 = (bf16[256,8192]{1,0:T(8,128)(2,1)S(1)}, bf16[256,8192]{1,0:T(8,128)(2,1)}, u32[]{:S(2)}) copy-start(bf16[256,8192]{1,0:T(8,128)(2,1)} %param.25) | copy-start | bytes 12582916
  288.3 4.7 %collective-permute-start.3 = (f32[192,256]{1,0:T(8,128)S(1)}, f32[192,256]{1,0:T(8,128)S(1)}, u32[]{:S(2)}, u32[]{:S(2)}) collective-permute-start(f32[192,256]{1,0:T(8,128)S(1)} %slice_select_fusion), channel_id=1, source_target_pairs={{0,64},{64,0},{1,65},{65,1},{2,66},{66,2},{3,67},{67,3},{4,68},{68... | collective-permute-start | bytes 589832 | tf_op jit(solution)/shard_map/ppermute | solution.py:32
  293.1 22.0 %copy-start.1 = (bf16[128,8192]{1,0:T(8,128)(2,1)S(1)}, bf16[128,8192]{1,0:T(8,128)(2,1)}, u32[]{:S(2)}) copy-start(bf16[128,8192]{1,0:T(8,128)(2,1)} %param.22) | copy-start | bytes 6291460
  (15 other events, 57.0 us)

commit v2 on v1

v2 whole, which is shorter than its diff:
```python
import math

import jax
import jax.numpy as jnp
from jax import lax
from jax.experimental import pallas as pl
from jax.experimental.pallas import tpu as pltpu
from jax.sharding import Mesh, PartitionSpec as P

HD = 128
STEPS = 3
CACHE = 128
EPSILON = 1e-05
NEGATIVE = -1e30
CHIPS = ("z", "xl", "y")
EVERY = ("grp",) + CHIPS
PLANE = ("xl", "y")
F32 = jnp.float32
BF16 = jnp.bfloat16


RING = (0, -1, 1, 2)


def hop(array, across, first, second):
    sizes = [lax.axis_size(name) for name in EVERY]

    def index(*place):
        total = 0
        for at, size in zip(place, sizes):
            total = total * size + at % size
        return total

    pairs = []
    for core in range(sizes[0]):
        dz, dy = (second, first) if core == 0 else (first, second)
        for z in range(sizes[1]):
            for x in range(sizes[2]):
                for y in range(sizes[3]):
                    pairs.append(
                        (index(core, z, x, y), index(core, z + dz, x + across, y + dy))
                    )
    return lax.ppermute(array, EVERY, pairs)


def chip_order():
    z, x, y = (lax.axis_index(name) for name in CHIPS)
    sizes = [lax.axis_size(name) for name in CHIPS]
    core = lax.axis_index("grp")
    ring = jnp.array(RING, jnp.int32)
    second, first, flip = ring[:, None, None], ring[None, :, None], jnp.arange(2)[None, None, :]
    dz = jnp.where(core == 0, second, first)
    dy = jnp.where(core == 0, first, second)
    place = ((z + dz) % sizes[0] * sizes[1] + (x + flip) % sizes[1]) * sizes[2]
    return (place + (y + dy) % sizes[2]).reshape(-1).astype(jnp.int32)


def gather_chips(shard):
    two = jnp.stack([shard, hop(shard, 1, 0, 0)])
    eight = jnp.concatenate([two] + [hop(two, 0, -d, 0) for d in RING[1:]])
    return [eight] + [hop(eight, 0, 0, -d) for d in RING[1:]]


def scatter_chips(pieces):
    def total(own, others):
        result = own.astype(F32)
        for other in others:
            result = result + other.astype(F32)
        return result

    eight = total(pieces[0], [hop(p, 0, 0, d) for p, d in zip(pieces[1:], RING[1:])])
    sent = eight[2:].astype(BF16)
    two = total(
        eight[:2], [hop(sent[2 * i : 2 * i + 2], 0, d, 0) for i, d in enumerate(RING[1:])]
    )
    return two[0] + hop(two[1].astype(BF16), 1, 0, 0).astype(F32)


def swap_cores(array):
    return lax.ppermute(array, "grp", [(0, 1), (1, 0)])


def rotation(positions, first_pair, pair_count):
    pair_index = (first_pair + jnp.arange(pair_count)).astype(F32)
    frequency = jnp.exp(pair_index * (-2.0 * math.log(10000.0) / HD))
    angles = positions.astype(F32)[..., None] * frequency
    return jnp.cos(angles), jnp.sin(angles)


def attend(queries, keys, values, fresh_keys, fresh_values, lengths):
    rows, steps, group, size = queries.shape
    factor = 1.0 / math.sqrt(HD)
    flat = queries.reshape(rows, steps * group, size)
    cached = jnp.einsum("rqd,rdl->rql", flat, keys, preferred_element_type=F32)
    fresh = jnp.einsum("rqd,rnd->rqn", flat, fresh_keys, preferred_element_type=F32)
    visible = (jnp.arange(CACHE)[None, :] < lengths[:, None])[:, None, :]
    step_of = jnp.arange(steps * group) // group
    seen = (jnp.arange(steps)[None, :] <= step_of[:, None])[None]
    cached = jnp.where(visible, cached * factor, NEGATIVE)
    fresh = jnp.where(seen, fresh * factor, NEGATIVE)
    top = jnp.maximum(jnp.max(cached, -1, keepdims=True), jnp.max(fresh, -1, keepdims=True))
    cached = jnp.exp(cached - top)
    fresh = jnp.exp(fresh - top)
    total = jnp.sum(cached, -1, keepdims=True) + jnp.sum(fresh, -1, keepdims=True)
    cached = (cached / total).astype(BF16)
    fresh = (fresh / total).astype(BF16)
    out = jnp.einsum("rql,rdl->rqd", cached, values, preferred_element_type=F32)
    out = out + jnp.einsum("rqn,rnd->rqd", fresh, fresh_values, preferred_element_type=F32)
    return out.astype(BF16).reshape(rows, steps, group, size)


VMEM = pltpu.VMEM
ACROSS = (((1,), (1,)), ((), ()))


def call(kernel, out_shapes, scratch, scalars, *arrays):
    in_specs = [pl.BlockSpec(memory_space=pltpu.SMEM)] * len(scalars)
    in_specs += [pl.BlockSpec(memory_space=VMEM)] * len(arrays)
    many = isinstance(out_shapes, (list, tuple))
    out_specs = pl.BlockSpec(memory_space=VMEM)
    return pl.pallas_call(
        kernel,
        out_shape=out_shapes,
        in_specs=in_specs,
        out_specs=[out_specs] * len(out_shapes) if many else out_specs,
        scratch_shapes=scratch,
        compiler_params=pltpu.CompilerParams(vmem_limit_bytes=40 * 2**20),
    )(*scalars, *arrays)


def lay_out(pieces, table, offset, width, lay):
    total = jnp.zeros((pieces[0].shape[1], width), F32)
    start = 0
    for piece in pieces:

        def step(i, total, piece=piece, start=start):
            return total + lay(piece[i, :, offset : offset + width], table[start + i])

        total = lax.fori_loop(0, piece.shape[0], step, total)
        start += piece.shape[0]
    return jnp.sum(total, axis=1, keepdims=True)


def column(t, width):
    return pl.ds(pl.multiple_of(t * width, width), width)


def lay_gained(pieces, table, offset, gain, laid):
    width = gain.shape[2]

    def lay(block, t):
        values = block.astype(F32)
        laid[:, column(t, width)] = (values * gain[t]).astype(BF16)
        return values * values

    return lay_out(pieces, table, offset, width, lay)


def lay_final(pieces, table, offset, inverse, laid):
    width = inverse.shape[2]

    def lay(block, t):
        laid[:, column(t, width)] = block
        values = block.astype(F32) * inverse[t]
        return values * values

    return lay_out(pieces, table, offset, width, lay)


def swap_pairs(values):
    lanes = values.shape[1]
    lane = lax.broadcasted_iota(jnp.int32, values.shape, 1)
    after = pltpu.roll(values, lanes - 1, 1)
    before = pltpu.roll(values, 1, 1)
    return jnp.where(lane % 2 == 0, after, before)


def project_base(pieces, table, core, gain, query, query_other, kv, kv_other):
    rows = pieces[0].shape[1]
    half = query_other.shape[0]
    wide = query.shape[1]
    slim = kv.shape[0]

    def kernel(table, core, *refs):
        parts = refs[: len(pieces)]
        gain, query, query_other, kv, kv_other, mine, theirs, laid, slot = refs[len(pieces) :]
        squares = lay_gained(parts, table, 0, gain, laid)
        values = laid[...]
        start = pl.multiple_of(core[0] * half, half)
        slot[...] = jnp.zeros_like(slot)
        lane = lax.broadcasted_iota(jnp.int32, slot.shape, 1)
        mine[:, :wide] = jnp.dot(
            values, query[pl.ds(start, half), :], preferred_element_type=F32
        )
        theirs[:, :wide] = jnp.dot(values, query_other[...], preferred_element_type=F32)
        slot[:, :slim] = lax.dot_general(
            values, kv[:, pl.ds(start, half)], ACROSS, preferred_element_type=F32
        )
        mine[:, wide:] = jnp.where(lane < slim, slot[...], squares)
        slot[:, :slim] = lax.dot_general(
            values, kv_other[...], ACROSS, preferred_element_type=F32
        )
        theirs[:, wide:] = jnp.where(lane < slim, slot[...], squares)

    shape = jax.ShapeDtypeStruct((rows, 2 * wide), F32)
    scratch = [VMEM((rows, half), BF16), VMEM((rows, wide), F32)]
    return call(
        kernel, [shape, shape], scratch, [table, core],
        *pieces, gain, query, query_other, kv, kv_other,
    )


def finish_base(mine, theirs, cosine, sine, features, slice_width):
    rows, lanes = mine.shape
    wide = lanes // 2

    def kernel(mine, theirs, cosine, sine, out):
        values = mine[...] + theirs[...]
        squares = values[:, lanes - 1 : lanes]
        scaling = lax.rsqrt(squares * (1.0 / features) + EPSILON)
        turned = scaling * (values * cosine[...] + swap_pairs(values) * sine[...])
        turned = turned.astype(BF16)
        source = lax.broadcasted_iota(jnp.int32, (wide, 2 * wide), 0)
        lane = lax.broadcasted_iota(jnp.int32, (wide, 2 * wide), 1)
        wanted = lane % slice_width + jnp.where(lane < wide, 0, slice_width)
        repeat = jnp.where(source == wanted, 1.0, 0.0).astype(BF16)
        out[:, :wide] = turned[:, :wide]
        out[:, wide:] = jnp.dot(
            turned[:, wide:], repeat, preferred_element_type=F32
        ).astype(BF16)

    shape = jax.ShapeDtypeStruct((rows, 3 * wide), BF16)
    return call(kernel, shape, [], [], mine, theirs, cosine, sine)


def attend_base(packed, cache, lengths, slice_width):
    shares, lined, lanes = packed.shape
    wide = lanes // 3
    part_rows = cache.shape[2]
    group = wide // slice_width
    queries = STEPS * group
    factor = 1.0 / math.sqrt(HD)

    def kernel(lengths, packed, cache, out, slot):
        sub = lax.broadcasted_iota(jnp.int32, (group, shares * wide), 0)
        lane = lax.broadcasted_iota(jnp.int32, (group, shares * wide), 1)
        own = lane % wide // slice_width == sub
        place = lax.broadcasted_iota(jnp.int32, (queries, CACHE), 1)
        fresh_place = lax.broadcasted_iota(jnp.int32, (queries, 16), 1)
        step_of = lax.broadcasted_iota(jnp.int32, (queries, 16), 0) // group
        seen = (fresh_place <= step_of) & (fresh_place < STEPS)
        blocks = [packed[c].astype(F32) for c in range(shares)]
        empty = jnp.zeros((16 - STEPS, shares * wide), F32)

        def line(row, start):
            return jnp.concatenate(
                [block[row : row + 1, start : start + wide] for block in blocks], axis=1
            )

        for r in range(part_rows):
            lines = [s * part_rows + r for s in range(STEPS)]
            asked = jnp.concatenate(
                [jnp.where(own, line(i, 0), 0.0) for i in lines], axis=0
            ).astype(BF16)
            keys = jnp.concatenate([line(i, wide) for i in lines] + [empty], 0).astype(BF16)
            values = jnp.concatenate([line(i, 2 * wide) for i in lines] + [empty], 0).astype(BF16)
            kept_keys = jnp.concatenate(
                [cache[c, 0, r] for c in range(shares) for _ in range(group)], axis=0
            )
            kept_values = jnp.concatenate(
                [cache[c, 1, r] for c in range(shares) for _ in range(group)], axis=0
            )
            cached = jnp.dot(asked, kept_keys, preferred_element_type=F32) * factor
            fresh = lax.dot_general(asked, keys, ACROSS, preferred_element_type=F32) * factor
            cached = jnp.where(place < lengths[r], cached, NEGATIVE)
            fresh = jnp.where(seen, fresh, NEGATIVE)
            top = jnp.maximum(
                jnp.max(cached, axis=1, keepdims=True), jnp.max(fresh, axis=1, keepdims=True)
            )
            cached = jnp.exp(cached - top)
            fresh = jnp.exp(fresh - top)
            total = jnp.sum(cached, axis=1, keepdims=True) + jnp.sum(fresh, axis=1, keepdims=True)
            cached = (cached / total).astype(BF16)
            fresh = (fresh / total).astype(BF16)
            result = lax.dot_general(cached, kept_values, ACROSS, preferred_element_type=F32)
            result = result + jnp.dot(fresh, values, preferred_element_type=F32)
            for s in range(STEPS):
                part = jnp.where(own, result[s * group : (s + 1) * group], 0.0)
                part = jnp.sum(part, axis=0, keepdims=True)
                for c in range(shares):
                    slot[c, lines[s] : lines[s] + 1, :] = part[:, c * wide : (c + 1) * wide]
        out[...] = slot[...].astype(BF16)

    shape = jax.ShapeDtypeStruct((shares, lined, wide), BF16)
    return call(kernel, shape, [VMEM((shares, lined, wide), F32)], [lengths], packed, cache)


def project_small(pieces, table, gain, projections, cosine, sine):
    rows = pieces[0].shape[1]
    features = projections.shape[1]
    wide = projections.shape[2]

    def kernel(table, *refs):
        parts = refs[: len(pieces)]
        gain, projections, cosine, sine, out, laid = refs[len(pieces) :]
        squares = lay_gained(parts, table, gain.shape[2], gain, laid)
        scaling = lax.rsqrt(squares * (1.0 / features) + EPSILON)
        for i in range(3):
            values = jnp.dot(laid[...], projections[i], preferred_element_type=F32) * scaling
            if i < 2:
                values = values * cosine[...] + swap_pairs(values) * sine[...]
            out[i] = values.astype(BF16)

    shape = jax.ShapeDtypeStruct((3, rows, wide), BF16)
    return call(
        kernel, shape, [VMEM((rows, features), BF16)], [table],
        *pieces, gain, projections, cosine, sine,
    )


def mix(heads, heads_other, small_heads, table, core, output, output_other, small_output, width):
    rows = heads.shape[0]
    count = table.shape[0]
    pieces = len(RING)
    each = count // pieces

    def kernel(table, core, heads, heads_other, small_heads, output, output_other, small_output,
               *outs):
        both = jnp.concatenate([heads[...], heads_other[...]], axis=1)
        small = small_heads[...]
        for piece in (3, 1, 2, 0):
            for i in range(each):
                t = table[piece * each + i]
                weights = jnp.concatenate(
                    [output[:, column(core[0] * count + t, width)],
                     output_other[:, column(t, width)]],
                    axis=0,
                )
                outs[piece][i, :, :width] = jnp.dot(
                    both, weights, preferred_element_type=F32
                ).astype(BF16)
                outs[piece][i, :, width:] = jnp.dot(
                    small, small_output[:, column(t, width)], preferred_element_type=F32
                ).astype(BF16)

    shape = jax.ShapeDtypeStruct((each, rows, 2 * width), BF16)
    return call(
        kernel, [shape] * pieces, [], [table, core],
        heads, heads_other, small_heads, output, output_other, small_output,
    )


def unembed_base(pieces, table, core, inverse, unembed, unembed_other):
    rows = pieces[0].shape[1]
    vocab, half = unembed_other.shape

    def kernel(table, core, *refs):
        parts = refs[: len(pieces)]
        inverse, unembed, unembed_other, mine, theirs, squares, laid = refs[len(pieces) :]
        squares[...] = jnp.broadcast_to(lay_final(parts, table, 0, inverse, laid), squares.shape)
        start = pl.multiple_of(core[0] * half, half)
        mine[...] = lax.dot_general(
            laid[...], unembed[:, pl.ds(start, half)], ACROSS, preferred_element_type=F32
        )
        theirs[...] = lax.dot_general(
            laid[...], unembed_other[...], ACROSS, preferred_element_type=F32
        )

    shape = jax.ShapeDtypeStruct((rows, vocab), F32)
    return call(
        kernel, [shape, shape, jax.ShapeDtypeStruct((rows, 128), F32)],
        [VMEM((rows, half), BF16)], [table, core],
        *pieces, inverse, unembed, unembed_other,
    )


def unembed_small(pieces, table, core, inverse, unembed):
    rows = pieces[0].shape[1]
    vocab, features = unembed.shape

    def kernel(table, core, *refs):
        parts = refs[: len(pieces)]
        inverse, unembed, out, laid = refs[len(pieces) :]
        squares = lay_final(parts, table, inverse.shape[2], inverse, laid)
        scaling = lax.rsqrt(squares * (1.0 / features) + EPSILON)
        scaling = jnp.where(core[0] == 0, scaling, -scaling)
        out[...] = scaling * lax.dot_general(
            laid[...], unembed[...], ACROSS, preferred_element_type=F32
        )

    shape = jax.ShapeDtypeStruct((rows, vocab), F32)
    return call(
        kernel, shape, [VMEM((rows, features), BF16)], [table, core],
        *pieces, inverse, unembed,
    )


def body(
    base_inputs,
    small_inputs,
    base_norm_gain,
    base_query,
    base_keys_values,
    base_output,
    base_cache,
    base_final_gain,
    base_unembed,
    small_norm_gain,
    small_projections,
    small_output,
    small_cache,
    small_final_gain,
    small_unembed,
    lengths,
    next_tokens,
):
    rows = lengths.shape[0]
    every_row = STEPS * rows
    chips = lax.axis_size(CHIPS)
    shares = lax.axis_size(PLANE)
    core = lax.axis_index("grp")
    chip = lax.axis_index(CHIPS)
    block = core * chips + chip
    share = lax.axis_index(PLANE)
    width = base_inputs.shape[2]
    slice_width = base_keys_values.shape[2]
    wide = base_query.shape[1]
    group = wide // slice_width
    part_rows = rows // shares
    vocab_width = base_unembed.shape[0]
    features = base_query.shape[0]
    half = features // 2
    positions = lengths.reshape(shares, 1, part_rows) + jnp.arange(STEPS)[None, :, None]
    positions = positions.reshape(every_row)
    core_index = core.reshape(1).astype(jnp.int32)
    table = chip_order()

    def by_share(array):
        array = array.reshape((STEPS, shares, part_rows) + array.shape[2:])
        return array.swapaxes(0, 1).reshape((every_row,) + array.shape[3:])

    shard = jnp.concatenate([by_share(base_inputs), by_share(small_inputs[0])], axis=-1)
    inputs = gather_chips(shard)

    def send_half(array, axis):
        return swap_cores(lax.dynamic_slice_in_dim(array, (1 - core) * half, half, axis))

    kv = base_keys_values.transpose(0, 2, 1).reshape(2 * slice_width, features)
    query_other = send_half(base_query, 0)
    kv_other = send_half(kv, 1)
    output_other = send_half(base_output, 1)
    unembed_other = send_half(base_unembed, 1)

    cache = base_cache.reshape(2, shares, part_rows, slice_width, CACHE).transpose(1, 0, 2, 3, 4)
    cache, _ = lax.optimization_barrier((cache, inputs[0]))
    cache = lax.all_to_all(cache, PLANE, 0, 0, tiled=True)

    def by_chip(gain):
        return gain.reshape(chips, 1, width)

    def half_of(gain):
        return by_chip(lax.dynamic_slice_in_dim(gain, core * half, half))

    def turn(first_pair, pair_count, copies):
        cosine, sine = rotation(positions, first_pair, pair_count)
        cosine = jnp.repeat(cosine, 2, axis=-1)
        sine = jnp.stack([-sine, sine], axis=-1).reshape(cosine.shape)
        return jnp.tile(cosine, (1, copies)), jnp.tile(sine, (1, copies))

    cosine, sine = turn(share * (slice_width // 2), slice_width // 2, group + 1)
    ones = jnp.ones((every_row, slice_width), F32)
    rest = jnp.zeros((every_row, wide - 2 * slice_width), F32)
    cosine = jnp.concatenate([cosine, ones, rest], axis=-1)
    sine = jnp.concatenate([sine, 0.0 * ones, rest], axis=-1)

    mine, theirs = project_base(
        inputs, table, core_index, half_of(base_norm_gain),
        base_query, query_other, kv, kv_other,
    )
    packed = finish_base(mine, swap_cores(theirs), cosine, sine, features, slice_width)
    packed = packed.reshape(shares, STEPS * part_rows, 3 * wide)
    packed = lax.all_to_all(packed, PLANE, 0, 0, tiled=True)
    part_lengths = lax.dynamic_slice_in_dim(lengths, share * part_rows, part_rows)
    heads = attend_base(packed, cache, part_lengths, slice_width)
    heads = lax.all_to_all(heads, PLANE, 0, 0, tiled=True).reshape(every_row, wide)

    later, _ = lax.optimization_barrier((inputs, theirs))
    cosine, sine = turn(0, HD // 2, 1)
    small_q, small_k, small_v = (
        array.reshape(shares, STEPS, part_rows, HD).swapaxes(1, 2).reshape(rows, STEPS, HD)
        for array in project_small(
            later, table, by_chip(small_norm_gain[0]), small_projections[0],
            cosine, sine,
        )
    )
    small_heads = attend(
        small_q[:, :, None], small_cache[0, 0], small_cache[0, 1], small_k, small_v, lengths
    )
    small_heads = small_heads.reshape(shares, part_rows, STEPS, HD).swapaxes(1, 2)
    small_heads = small_heads.reshape(every_row, HD)

    sums = scatter_chips(
        mix(
            heads, swap_cores(heads), small_heads, table, core_index, base_output, output_other,
            small_output[0], width,
        )
    )
    base_gain = lax.dynamic_slice_in_dim(base_final_gain, block * width, width)
    small_gain = lax.dynamic_slice_in_dim(small_final_gain[0], chip * width, width)
    hidden = shard.astype(F32) + sums
    finals = gather_chips((hidden * jnp.concatenate([base_gain, small_gain])).astype(BF16))
    mine, theirs, squares = unembed_base(
        finals, table, core_index, 1.0 / half_of(base_final_gain), base_unembed, unembed_other,
    )
    later, _ = lax.optimization_barrier((finals, theirs))
    small_logits = unembed_small(
        later, table, core_index, 1.0 / by_chip(small_final_gain[0]),
        small_unembed[0].reshape(-1, small_unembed.shape[3]),
    )
    low, high = small_logits[:, :vocab_width], small_logits[:, vocab_width:]
    mean = (squares + swap_cores(squares))[:, :1] * (1.0 / features)
    steered = (mine + swap_cores(theirs)) * lax.rsqrt(mean + EPSILON)
    steered = steered + jnp.where(core == 0, low, high)
    steered = steered + swap_cores(jnp.where(core == 0, high, low))

    local_max = jnp.max(steered, axis=-1)
    local_sum = jnp.sum(jnp.exp(steered - local_max[:, None]), axis=-1)
    local_token = by_share(next_tokens) - block * vocab_width
    hit = jnp.arange(vocab_width)[None, :] == local_token[:, None]
    picked = jnp.sum(jnp.where(hit, steered, 0.0), axis=-1)
    triple = jnp.stack([local_max, local_sum, picked])
    count = lax.axis_size(EVERY)
    triples = lax.all_to_all(
        jnp.broadcast_to(triple[None], (count,) + triple.shape), EVERY, 0, 0, tiled=True
    )
    top = jnp.max(triples[:, 0], axis=0)
    total = jnp.sum(triples[:, 1] * jnp.exp(triples[:, 0] - top[None]), axis=0)
    log_norm = top + jnp.log(total)
    chosen = jnp.sum(triples[:, 2], axis=0) - log_norm
    log_probs = (steered - log_norm[:, None]).reshape(shares, STEPS, part_rows, vocab_width)
    log_probs = log_probs.swapaxes(0, 1).reshape(STEPS, rows, vocab_width)
    return log_probs, jnp.sum(chosen.reshape(shares, STEPS, part_rows), axis=1).reshape(rows)


def solution(mesh):
    devices = mesh.devices
    fine = Mesh(devices.reshape(2, 4, 2, 4, 2), ("grp", "z", "xl", "y", "dp"))
    placed = (
        P(None, "dp", EVERY),
        P("grp", None, "dp", CHIPS),
        P(),
        P(None, EVERY),
        P(None, None, EVERY),
        P(EVERY, None),
        P(None, "dp", EVERY, None),
        P(),
        P(EVERY, None),
        P("grp", None),
        P("grp", None, None, CHIPS),
        P("grp", CHIPS, None),
        P("grp", None, "dp", CHIPS, None),
        P("grp", None),
        P("grp", None, CHIPS, None),
        P("dp"),
        P(None, "dp"),
    )
    return jax.shard_map(
        body,
        mesh=fine,
        in_specs=placed,
        out_specs=(P(None, "dp", EVERY), P("dp")),
        check_vma=False,
    )
```

time: 321 us -> 205 us (0.64); the launches traced: 316 us -> 204 us
  local copies, waits for them, and re-layouts: 72.6 us -> 23 us
  waiting for transfers between devices: 110 us -> 73.8 us
  matrix products: 34.8 us -> 4.61 us
  Pallas kernels: 0 us -> 25.3 us
  other arithmetic: 31.3 us -> 8.85 us
    all_to_all x4 -> x1, waiting for transfers between devices: 106 us -> 4.81 us  [body(): lax.all_to_all(heads, PLANE, 0, 0, tiled=True).reshape(every_row, wide)]
    ppermute x0 -> x21, waiting for transfers between devices: none -> 65.7 us  [hop(): return lax.ppermute(array, EVERY, pairs)]
    convert_element_type x9 -> x2, local copies, waits for them, and re-layouts: 32.4 us -> 0.11 us  [the longest x1 0.09 us: rotation(): angles = positions.astype(F32)[..., None] * frequency]
    dot_general x10 -> x0, matrix products: 27.9 us -> none  [the longest x3 7.02 us: body(): jnp.dot(small_normed, small_projections[0, i], preferred_element_type=F32)]
    pallas_call x0 -> x7, Pallas kernels: none -> 25.3 us  [call(): pl.pallas_call(kernel, out_shape=out_shapes, in_specs=in_specs, out_specs...]
    all_to_all x4 -> x1, starting transfers between devices: 27 us -> 3.35 us  [body(): lax.all_to_all(heads, PLANE, 0, 0, tiled=True).reshape(every_row, wide)]
    ppermute x0 -> x21, starting transfers between devices: none -> 23.5 us  [hop(): return lax.ppermute(array, EVERY, pairs)]
    dot_general x9 -> x0, local copies, waits for them, and re-layouts: 18.4 us -> none  [the longest x5 8.98 us: body(): jnp.dot(small_normed, small_projections[0, i], preferred_element_type=F32)]
  transfers between devices with their start and end apart: 10 -> 33, of which waited for: 5 -> 17; matrix products, arithmetic and copies ran while one was open for 20% -> 12% of each run, Pallas kernels for 0% -> 9%
where the time goes in v2:
time: 205 us; the launch traced here: 204 us
  waiting for transfers between devices  73.8 us (36%)
  starting transfers between devices  52.2 us (25%)
  Pallas kernels  25.3 us (12%)
  local copies, waits for them, and re-layouts  23 us (11%)
  blocking collectives  14.7 us (7%)
  other arithmetic  8.85 us (4%)
  matrix products  4.61 us (2%)
    ppermute x21, waiting for transfers between devices, hop(): return lax.ppermute(array, EVERY, pairs)  65.7 us
    pallas_call x7, Pallas kernels, call(): pl.pallas_call(kernel, out_shape=out_shapes, in_specs=in_specs, out_specs...  25.3 us
    ppermute x21, starting transfers between devices, hop(): return lax.ppermute(array, EVERY, pairs)  23.5 us
    ppermute x9, starting transfers between devices, swap_cores(): return lax.ppermute(array, 'grp', [(0, 1), (1, 0)])  18.2 us
    all_to_all x1, blocking collectives, body(): lax.all_to_all(jnp.broadcast_to(triple[None], (count,) + triple.shape), E...  14.7 us
    dynamic_slice x4, local copies, waits for them, and re-layouts, send_half(): lax.dynamic_slice_in_dim(array, (1 - core) * half, half, axis)  6.5 us
    unnamed x56, local copies, waits for them, and re-layouts  6.2 us
    all_to_all x1, waiting for transfers between devices, body(): lax.all_to_all(heads, PLANE, 0, 0, tiled=True).reshape(every_row, wide)  4.81 us
  transfers between devices with their start and end apart: 33, of which 17 were waited for; matrix products, arithmetic and copies ran while one was open for 12% of the time, Pallas kernels for 9%

profile of v2, /device:TPU:1, one launch (start us, length us, event | category | flops | bytes accessed | tf_op | source)
XLA Modules:
  0.0 203.7 jit_solution(8254480233936003417)
XLA Ops:
  3.0 2.0 %collective-permute-start = (bf16[192,256]{1,0:T(8,128)(2,1)}, bf16[192,256]{1,0:T(8,128)(2,1)S(1)}, u32[]{:S(2)}, u32[]{:S(2)}) collective-permute-start(bf16[192,256]{1,0:T(8,128)(2,1)} %get-tuple-element.59), channel_id=1, source_target_pairs={{0,8},{2,10},{4,12},{6,14},{8,0},{10,2},{12,4},{14,6},{16,24},{18,... | collective-permute-start | bytes 294920 | tf_op jit(solution)/shard_map/ppermute | solution.py:43
  7.7 2.3 %constant_dynamic-slice_fusion.4 = bf16[4096,128]{1,0:T(8,128)(2,1)} fusion(bf16[8192,128]{1,0:T(8,128)(2,1)} %refs_5_.2, s32[]{:T(128)S(6)} %select_n.111), kind=kLoop, calls=%fused_computation.97 | loop fusion | bytes 2097156 | tf_op jit(solution)/shard_map/dynamic_slice | solution.py:446
  14.5 2.2 %collective-permute-start.2 = (bf16[2,192,256]{2,1,0:T(8,128)(2,1)S(1)}, bf16[2,192,256]{2,1,0:T(8,128)(2,1)S(1)}, u32[]{:S(2)}, u32[]{:S(2)}) collective-permute-start(bf16[2,192,256]{2,1,0:T(8,128)(2,1)S(1)} %pad_maximum_fusion), channel_id=1, source_target_pairs={{0,6},{2,0},{4,2},{6,4},{8,14},{10,8},{12,10},{14,12},{16,22},{18,... | collective-permute-start | bytes 589832 | tf_op jit(solution)/shard_map/ppermute | solution.py:43
  35.4 3.5 %all-to-all-start.1 = ((bf16[8,2,8,16,128]{4,3,2,1,0:T(8,128)(2,1)}), bf16[8,2,8,16,128]{4,3,2,1,0:T(8,128)(2,1)S(1)}, u32[]{:S(2)}, u32[]{:S(2)}) async-start(bf16[8,2,8,16,128]{4,3,2,1,0:T(8,128)(2,1)} %bitcast.128), calls=%async_computation.1 | async-start | bytes 1048576 | tf_op jit(solution)/shard_map/all_to_all | solution.py:456
  38.9 2.3 %collective-permute-start.11 = (bf16[128,4096]{1,0:T(8,128)(2,1)}, bf16[128,4096]{1,0:T(8,128)(2,1)}, u32[]{:S(2)}, u32[]{:S(2)}) collective-permute-start(bf16[128,4096]{1,0:T(8,128)(2,1)} %constant_dynamic-slice_fusion.2), channel_id=1, source_target_pairs={{0,64},{64,0},{1,65},{65,1},{2,66},{66,2},{3,67},{67,3},{4,68},{68... | collective-permute-start | bytes 3145736 | tf_op jit(solution)/shard_map/ppermute | solution.py:80
  41.2 4.1 %collective-permute-done.5.refs_2_ = bf16[8,192,256]{2,1,0:T(8,128)(2,1)} collective-permute-done((bf16[8,192,256]{2,1,0:T(8,128)(2,1)S(1)}, bf16[8,192,256]{2,1,0:T(8,128)(2,1)}, u32[]{:S(2)}, u32[]{:S(2)}) %collective-permute-start.5) | collective-permute-done | bytes 786464 | tf_op jit(solution)/shard_map/ppermute | solution.py:43
  49.3 5.4 %shard_map.185 = (f32[192,256]{1,0:T(8,128)S(1)}, f32[192,256]{1,0:T(8,128)}) custom-call(s32[32]{0:T(128)S(1)} %add.229.table, s32[1]{0:T(128)} %bitcast.core, bf16[8,192,256]{2,1,0:T(8,128)(2,1)S(1)} %constant_dynamic-update-slice_fusion.refs_0_, bf16[8,192,256]{2,1,0:T(8,128)(2,1)} %collective-permute-done.4.refs_1_, ...), custom_call_target="tpu_custom_call" | custom-call | tf_op jit(solution)/shard_map/pallas_call | solution.py:121
  55.8 4.0 %shard_map.188 = bf16[3,192,128]{2,1,0:T(8,128)(2,1)S(1)} custom-call(s32[32]{0:T(128)S(1)} %add.229.table, bf16[8,192,256]{2,1,0:T(8,128)(2,1)S(1)} %constant_dynamic-update-slice_fusion.refs_0_, bf16[8,192,256]{2,1,0:T(8,128)(2,1)} %collective-permute-done.4.refs_1_, bf16[8,192,256]{2,1,0:T(8,128)(2,1)} %collective-permute-done.5.refs_2_, ...), custom_call_target="tpu_custom_call" | custom-call | tf_op jit(solution)/shard_map/pallas_call | solution.py:121
  65.1 3.6 %all-to-all-start = ((bf16[8,24,384]{2,1,0:T(8,128)(2,1)}), bf16[8,24,384]{2,1,0:T(8,128)(2,1)S(1)}, u32[]{:S(2)}, u32[]{:S(2)}) async-start(bf16[8,24,384]{2,1,0:T(8,128)(2,1)} %bitcast.15), calls=%async_computation | async-start | bytes 294912 | tf_op jit(solution)/shard_map/all_to_all | solution.py:482
  68.7 2.9 %fusion = f32[64,3,128]{2,1,0:T(4,128)S(1)} fusion(bf16[1,2,64,128,128]{4,3,2,1,0:T(8,128)(2,1)} %param.30, f32[64,3,128]{2,1,0:T(4,128)} %get-tuple-element.69, f32[64,3]{1,0:T(8,128)S(1)} %add.240, f32[64,3]{1,0:T(8,128)S(1)} %max.8), kind=kOutput, calls=%fused_computation | convolution fusion | flops 6365184 | bytes 2328064 | tf_op jit(solution)/shard_map/rql,rdl->rqd/dot_general | solution.py:107
  71.7 2.7 %all-to-all-done.packed = bf16[8,24,384]{2,1,0:T(8,128)(2,1)S(1)} async-done(((bf16[8,24,384]{2,1,0:T(8,128)(2,1)}), bf16[8,24,384]{2,1,0:T(8,128)(2,1)S(1)}, u32[]{:S(2)}, u32[]{:S(2)}) %all-to-all-start) | async-done | bytes 147488 | tf_op jit(solution)/shard_map/all_to_all | solution.py:482
  74.3 3.7 %shard_map.187 = bf16[8,24,128]{2,1,0:T(8,128)(2,1)} custom-call(s32[8]{0:T(128)S(1)} %dynamic_slice.29.lengths, bf16[8,24,384]{2,1,0:T(8,128)(2,1)S(1)} %all-to-all-done.packed, bf16[8,2,8,16,128]{4,3,2,1,0:T(8,128)(2,1)S(1)} %all-to-all-done.1.cache), custom_call_target="tpu_custom_call" | custom-call | tf_op jit(solution)/shard_map/pallas_call | solution.py:121
  78.1 3.3 %all-to-all-start.2 = ((bf16[8,24,128]{2,1,0:T(8,128)(2,1)}), bf16[8,24,128]{2,1,0:T(8,128)(2,1)S(1)}, u32[]{:S(2)}, u32[]{:S(2)}) async-start(bf16[8,24,128]{2,1,0:T(8,128)(2,1)} %shard_map.187), calls=%async_computation.2 | async-start | bytes 98304 | tf_op jit(solution)/shard_map/all_to_all | solution.py:485
  81.7 4.8 %all-to-all-done.2 = bf16[8,24,128]{2,1,0:T(8,128)(2,1)S(1)} async-done(((bf16[8,24,128]{2,1,0:T(8,128)(2,1)}), bf16[8,24,128]{2,1,0:T(8,128)(2,1)S(1)}, u32[]{:S(2)}, u32[]{:S(2)}) %all-to-all-start.2) | async-done | bytes 49184 | tf_op jit(solution)/shard_map/all_to_all | solution.py:485
  86.5 3.0 %collective-permute-start.10 = (bf16[192,128]{1,0:T(8,128)(2,1)S(1)}, bf16[192,128]{1,0:T(8,128)(2,1)S(1)}, u32[]{:S(2)}, u32[]{:S(2)}) collective-permute-start(bf16[192,128]{1,0:T(8,128)(2,1)S(1)} %bitcast.123), channel_id=1, source_target_pairs={{0,64},{64,0},{1,65},{65,1},{2,66},{66,2},{3,67},{67,3},{4,68},{68... | collective-permute-start | bytes 147464 | tf_op jit(solution)/shard_map/ppermute | solution.py:80
  91.6 2.7 %shard_map.189 = (bf16[8,192,256]{2,1,0:T(8,128)(2,1)S(1)}, bf16[8,192,256]{2,1,0:T(8,128)(2,1)S(1)}, bf16[8,192,256]{2,1,0:T(8,128)(2,1)S(1)}, bf16[8,192,256]{2,1,0:T(8,128)(2,1)S(1)}) custom-call(s32[32]{0:T(128)S(1)} %add.229.table, s32[1]{0:T(128)} %bitcast.core, bf16[192,128]{1,0:T(8,128)(2,1)S(1)} %bitcast.124, ...), custom_call_target="tpu_custom_call" | custom-call | tf_op jit(solution)/shard_map/pallas_call | solution.py:121
  96.6 8.8 %collective-permute-done.12 = bf16[8,192,256]{2,1,0:T(8,128)(2,1)S(1)} collective-permute-done((bf16[8,192,256]{2,1,0:T(8,128)(2,1)S(1)}, bf16[8,192,256]{2,1,0:T(8,128)(2,1)S(1)}, u32[]{:S(2)}, u32[]{:S(2)}) %collective-permute-start.12) | collective-permute-done | bytes 786464 | tf_op jit(solution)/shard_map/ppermute | solution.py:43
  105.5 10.5 %collective-permute-done.13 = bf16[8,192,256]{2,1,0:T(8,128)(2,1)S(1)} collective-permute-done((bf16[8,192,256]{2,1,0:T(8,128)(2,1)S(1)}, bf16[8,192,256]{2,1,0:T(8,128)(2,1)S(1)}, u32[]{:S(2)}, u32[]{:S(2)}) %collective-permute-start.13) | collective-permute-done | bytes 786464 | tf_op jit(solution)/shard_map/ppermute | solution.py:43
  116.5 2.1 %collective-permute-start.15 = (bf16[2,192,256]{2,1,0:T(8,128)(2,1)S(1)}, bf16[2,192,256]{2,1,0:T(8,128)(2,1)S(1)}, u32[]{:S(2)}, u32[]{:S(2)}) collective-permute-start(bf16[2,192,256]{2,1,0:T(8,128)(2,1)S(1)} %get-tuple-element.50), channel_id=1, source_target_pairs={{0,6},{2,0},{4,2},{6,4},{8,14},{10,8},{12,10},{14,12},{16,22},{18,... | collective-permute-start | bytes 589832 | tf_op jit(solution)/shard_map/ppermute | solution.py:43
  121.4 2.5 %collective-permute-start.26 = (bf16[256,4096]{1,0:T(8,128)(2,1)}, bf16[256,4096]{1,0:T(8,128)(2,1)}, u32[]{:S(2)}, u32[]{:S(2)}) collective-permute-start(bf16[256,4096]{1,0:T(8,128)(2,1)} %constant_dynamic-slice_fusion), channel_id=1, source_target_pairs={{0,64},{64,0},{1,65},{65,1},{2,66},{66,2},{3,67},{67,3},{4,68},{68... | collective-permute-start | bytes 6291464 | tf_op jit(solution)/shard_map/ppermute | solution.py:80
  124.1 2.7 %collective-permute-done.16 = bf16[2,192,256]{2,1,0:T(8,128)(2,1)S(1)} collective-permute-done((bf16[2,192,256]{2,1,0:T(8,128)(2,1)S(1)}, bf16[2,192,256]{2,1,0:T(8,128)(2,1)S(1)}, u32[]{:S(2)}, u32[]{:S(2)}) %collective-permute-start.16) | collective-permute-done | bytes 196640 | tf_op jit(solution)/shard_map/ppermute | solution.py:43
  127.3 3.1 %collective-permute-done.18 = bf16[192,256]{1,0:T(8,128)(2,1)S(1)} collective-permute-done((bf16[192,256]{1,0:T(8,128)(2,1)S(1)}, bf16[192,256]{1,0:T(8,128)(2,1)S(1)}, u32[]{:S(2)}, u32[]{:S(2)}) %collective-permute-start.18) | collective-permute-done | bytes 98336 | tf_op jit(solution)/shard_map/ppermute | solution.py:43
  130.9 3.7 %collective-permute-done.19 = bf16[192,256]{1,0:T(8,128)(2,1)S(1)} collective-permute-done((bf16[192,256]{1,0:T(8,128)(2,1)S(1)}, bf16[192,256]{1,0:T(8,128)(2,1)S(1)}, u32[]{:S(2)}, u32[]{:S(2)}) %collective-permute-start.19) | collective-permute-done | bytes 98336 | tf_op jit(solution)/shard_map/ppermute | solution.py:43
  134.7 2.7 %collective-permute-start.21 = (bf16[2,192,256]{2,1,0:T(8,128)(2,1)S(1)}, bf16[2,192,256]{2,1,0:T(8,128)(2,1)S(1)}, u32[]{:S(2)}, u32[]{:S(2)}) collective-permute-start(bf16[2,192,256]{2,1,0:T(8,128)(2,1)S(1)} %pad_maximum_fusion.1), channel_id=1, source_target_pairs={{0,6},{2,0},{4,2},{6,4},{8,14},{10,8},{12,10},{14,12},{16,22},{18,... | collective-permute-start | bytes 589832 | tf_op jit(solution)/shard_map/ppermute | solution.py:43
  137.4 3.0 %collective-permute-done.20 = bf16[2,192,256]{2,1,0:T(8,128)(2,1)S(1)} collective-permute-done((bf16[2,192,256]{2,1,0:T(8,128)(2,1)S(1)}, bf16[2,192,256]{2,1,0:T(8,128)(2,1)S(1)}, u32[]{:S(2)}, u32[]{:S(2)}) %collective-permute-start.20) | collective-permute-done | bytes 196640 | tf_op jit(solution)/shard_map/ppermute | solution.py:43
  143.5 2.7 %collective-permute-start.24 = (bf16[8,192,256]{2,1,0:T(8,128)(2,1)S(1)}, bf16[8,192,256]{2,1,0:T(8,128)(2,1)S(1)}, u32[]{:S(2)}, u32[]{:S(2)}) collective-permute-start(bf16[8,192,256]{2,1,0:T(8,128)(2,1)S(1)} %constant_dynamic-update-slice_fusion.5.refs_0_), channel_id=1, source_target_pairs={{0,48},{2,50},{4,52},{6,54},{8,56},{10,58},{12,60},{14,62},{16,0},... | collective-permute-start | bytes 2359304 | tf_op jit(solution)/shard_map/ppermute | solution.py:43
  146.2 20.1 %collective-permute-done.23.refs_1_ = bf16[8,192,256]{2,1,0:T(8,128)(2,1)S(1)} collective-permute-done((bf16[8,192,256]{2,1,0:T(8,128)(2,1)S(1)}, bf16[8,192,256]{2,1,0:T(8,128)(2,1)S(1)}, u32[]{:S(2)}, u32[]{:S(2)}) %collective-permute-start.23) | collective-permute-done | bytes 786464 | tf_op jit(solution)/shard_map/ppermute | solution.py:43
  166.4 2.2 %copy-done.1 = bf16[256,8192]{1,0:T(8,128)(2,1)S(1)} copy-done((bf16[256,8192]{1,0:T(8,128)(2,1)S(1)}, bf16[256,8192]{1,0:T(8,128)(2,1)}, u32[]{:S(2)}) %copy-start.1) | copy-done | bytes 4194328
  168.5 4.7 %shard_map.190 = (f32[192,256]{1,0:T(8,128)S(1)}, f32[192,256]{1,0:T(8,128)}, f32[192,128]{1,0:T(8,128)}) custom-call(s32[32]{0:T(128)S(1)} %add.229.table, s32[1]{0:T(128)} %bitcast.core, bf16[8,192,256]{2,1,0:T(8,128)(2,1)S(1)} %constant_dynamic-update-slice_fusion.5.refs_0_, bf16[8,192,256]{2,1,0:T(8,128)(2,1)S(1)} %collective-permute-done.23.refs_1_, ...), custom_call_target="tpu_custom_call" | custom-call | tf_op jit(solution)/shard_map/pallas_call | solution.py:121
  173.3 7.7 %collective-permute-start.28 = (f32[192,128]{1,0:T(8,128)}, f32[192,128]{1,0:T(8,128)}, u32[]{:S(2)}, u32[]{:S(2)}) collective-permute-start(f32[192,128]{1,0:T(8,128)} %get-tuple-element.33), channel_id=1, source_target_pairs={{0,64},{64,0},{1,65},{65,1},{2,66},{66,2},{3,67},{67,3},{4,68},{68... | collective-permute-start | bytes 294920 | tf_op jit(solution)/shard_map/ppermute | solution.py:80
  181.3 2.9 %shard_map.191 = f32[192,512]{1,0:T(8,128)S(1)} custom-call(s32[32]{0:T(128)S(1)} %add.229.table, s32[1]{0:T(128)} %bitcast.core, bf16[8,192,256]{2,1,0:T(8,128)(2,1)S(1)} %constant_dynamic-update-slice_fusion.5.refs_0_, bf16[8,192,256]{2,1,0:T(8,128)(2,1)S(1)} %collective-permute-done.23.refs_1_, bf16[8,192,256]{2,1,0:T(8,128)(2,1)S(1)} %collective-permute-done.24.refs_2_, ...), custom_call_target="tpu_custom_call" | custom-call | tf_op jit(solution)/shard_map/pallas_call | solution.py:121
  187.3 14.7 %all_to_all.20 = f32[64,3,192]{2,1,0:T(4,128)S(1)} all-to-all(f32[64,3,192]{2,1,0:T(4,128)S(1)} %broadcast_in_dim.109), channel_id=1, replica_groups=mesh['grp'=2,'z'=4,'xl'=2,'y'=4,'dp'=2] {'grp','z','xl','y'}, dimensions={0} | all-to-all | bytes 294912 | tf_op jit(solution)/shard_map/all_to_all | solution.py:533
  (200 shorter events, 55.8 us)
Async XLA Ops:
  3.0 9.7 %collective-permute-start = (bf16[192,256]{1,0:T(8,128)(2,1)}, bf16[192,256]{1,0:T(8,128)(2,1)S(1)}, u32[]{:S(2)}, u32[]{:S(2)}) collective-permute-start(bf16[192,256]{1,0:T(8,128)(2,1)} %get-tuple-element.59), channel_id=1, source_target_pairs={{0,8},{2,10},{4,12},{6,14},{8,0},{10,2},{12,4},{14,6},{16,24},{18,... | collective-permute-start | bytes 294920 | tf_op jit(solution)/shard_map/ppermute | solution.py:43
  6.7 32.2 %collective-permute-start.8 = (bf16[32,4096]{1,0:T(8,128)(2,1)}, bf16[32,4096]{1,0:T(8,128)(2,1)}, u32[]{:S(2)}, u32[]{:S(2)}) collective-permute-start(bf16[32,4096]{1,0:T(8,128)(2,1)} %constant_dynamic-slice_fusion.3), channel_id=1, source_target_pairs={{0,64},{64,0},{1,65},{65,1},{2,66},{66,2},{3,67},{67,3},{4,68},{68... | collective-permute-start | bytes 786440 | tf_op jit(solution)/shard_map/ppermute | solution.py:80
  9.9 31.3 %collective-permute-start.7 = (bf16[4096,128]{1,0:T(8,128)(2,1)}, bf16[4096,128]{1,0:T(8,128)(2,1)}, u32[]{:S(2)}, u32[]{:S(2)}) collective-permute-start(bf16[4096,128]{1,0:T(8,128)(2,1)} %constant_dynamic-slice_fusion.4), channel_id=1, source_target_pairs={{0,64},{64,0},{1,65},{65,1},{2,66},{66,2},{3,67},{67,3},{4,68},{68... | collective-permute-start | bytes 3145736 | tf_op jit(solution)/shard_map/ppermute | solution.py:80
  12.8 6.9 %collective-permute-start.1 = (bf16[2,192,256]{2,1,0:T(8,128)(2,1)S(1)}, bf16[2,192,256]{2,1,0:T(8,128)(2,1)S(1)}, u32[]{:S(2)}, u32[]{:S(2)}) collective-permute-start(bf16[2,192,256]{2,1,0:T(8,128)(2,1)S(1)} %pad_maximum_fusion), channel_id=1, source_target_pairs={{0,2},{2,4},{4,6},{6,0},{8,10},{10,12},{12,14},{14,8},{16,18},{18,... | collective-permute-start | bytes 589832 | tf_op jit(solution)/shard_map/ppermute | solution.py:43
  14.5 6.9 %collective-permute-start.2 = (bf16[2,192,256]{2,1,0:T(8,128)(2,1)S(1)}, bf16[2,192,256]{2,1,0:T(8,128)(2,1)S(1)}, u32[]{:S(2)}, u32[]{:S(2)}) collective-permute-start(bf16[2,192,256]{2,1,0:T(8,128)(2,1)S(1)} %pad_maximum_fusion), channel_id=1, source_target_pairs={{0,6},{2,0},{4,2},{6,4},{8,14},{10,8},{12,10},{14,12},{16,22},{18,... | collective-permute-start | bytes 589832 | tf_op jit(solution)/shard_map/ppermute | solution.py:43
  16.7 6.5 %collective-permute-start.3 = (bf16[2,192,256]{2,1,0:T(8,128)(2,1)S(1)}, bf16[2,192,256]{2,1,0:T(8,128)(2,1)S(1)}, u32[]{:S(2)}, u32[]{:S(2)}) collective-permute-start(bf16[2,192,256]{2,1,0:T(8,128)(2,1)S(1)} %pad_maximum_fusion), channel_id=1, source_target_pairs={{0,4},{2,6},{4,0},{6,2},{8,12},{10,14},{12,8},{14,10},{16,20},{18,... | collective-permute-start | bytes 589832 | tf_op jit(solution)/shard_map/ppermute | solution.py:43
  23.2 18.0 %collective-permute-start.4 = (bf16[8,192,256]{2,1,0:T(8,128)(2,1)S(1)}, bf16[8,192,256]{2,1,0:T(8,128)(2,1)}, u32[]{:S(2)}, u32[]{:S(2)}) collective-permute-start(bf16[8,192,256]{2,1,0:T(8,128)(2,1)S(1)} %constant_dynamic-update-slice_fusion.refs_0_), channel_id=1, source_target_pairs={{0,16},{2,18},{4,20},{6,22},{8,24},{10,26},{12,28},{14,30},{16,32}... | collective-permute-start | bytes 2359304 | tf_op jit(solution)/shard_map/ppermute | solution.py:43
  24.3 21.0 %collective-permute-start.5 = (bf16[8,192,256]{2,1,0:T(8,128)(2,1)S(1)}, bf16[8,192,256]{2,1,0:T(8,128)(2,1)}, u32[]{:S(2)}, u32[]{:S(2)}) collective-permute-start(bf16[8,192,256]{2,1,0:T(8,128)(2,1)S(1)} %constant_dynamic-update-slice_fusion.refs_0_), channel_id=1, source_target_pairs={{0,48},{2,50},{4,52},{6,54},{8,56},{10,58},{12,60},{14,62},{16,0},... | collective-permute-start | bytes 2359304 | tf_op jit(solution)/shard_map/ppermute | solution.py:43
  26.0 20.6 %collective-permute-start.6 = (bf16[8,192,256]{2,1,0:T(8,128)(2,1)S(1)}, bf16[8,192,256]{2,1,0:T(8,128)(2,1)}, u32[]{:S(2)}, u32[]{:S(2)}) collective-permute-start(bf16[8,192,256]{2,1,0:T(8,128)(2,1)S(1)} %constant_dynamic-update-slice_fusion.refs_0_), channel_id=1, source_target_pairs={{0,32},{2,34},{4,36},{6,38},{8,40},{10,42},{12,44},{14,46},{16,48}... | collective-permute-start | bytes 2359304 | tf_op jit(solution)/shard_map/ppermute | solution.py:43
  35.4 29.6 %all-to-all-start.1 = ((bf16[8,2,8,16,128]{4,3,2,1,0:T(8,128)(2,1)}), bf16[8,2,8,16,128]{4,3,2,1,0:T(8,128)(2,1)S(1)}, u32[]{:S(2)}, u32[]{:S(2)}) async-start(bf16[8,2,8,16,128]{4,3,2,1,0:T(8,128)(2,1)} %bitcast.128), calls=%async_computation.1 | async-start | bytes 1048576 | tf_op jit(solution)/shard_map/all_to_all | solution.py:456
  38.9 50.8 %collective-permute-start.11 = (bf16[128,4096]{1,0:T(8,128)(2,1)}, bf16[128,4096]{1,0:T(8,128)(2,1)}, u32[]{:S(2)}, u32[]{:S(2)}) collective-permute-start(bf16[128,4096]{1,0:T(8,128)(2,1)} %constant_dynamic-slice_fusion.2), channel_id=1, source_target_pairs={{0,64},{64,0},{1,65},{65,1},{2,66},{66,2},{3,67},{67,3},{4,68},{68... | collective-permute-start | bytes 3145736 | tf_op jit(solution)/shard_map/ppermute | solution.py:80
  54.7 8.5 %collective-permute-start.9 = (f32[192,256]{1,0:T(8,128)}, f32[192,256]{1,0:T(8,128)}, u32[]{:S(2)}, u32[]{:S(2)}) collective-permute-start(f32[192,256]{1,0:T(8,128)} %get-tuple-element.21), channel_id=1, source_target_pairs={{0,64},{64,0},{1,65},{65,1},{2,66},{66,2},{3,67},{67,3},{4,68},{68... | collective-permute-start | bytes 589832 | tf_op jit(solution)/shard_map/ppermute | solution.py:80
  65.1 9.2 %all-to-all-start = ((bf16[8,24,384]{2,1,0:T(8,128)(2,1)}), bf16[8,24,384]{2,1,0:T(8,128)(2,1)S(1)}, u32[]{:S(2)}, u32[]{:S(2)}) async-start(bf16[8,24,384]{2,1,0:T(8,128)(2,1)} %bitcast.15), calls=%async_computation | async-start | bytes 294912 | tf_op jit(solution)/shard_map/all_to_all | solution.py:482
  78.1 8.4 %all-to-all-start.2 = ((bf16[8,24,128]{2,1,0:T(8,128)(2,1)}), bf16[8,24,128]{2,1,0:T(8,128)(2,1)S(1)}, u32[]{:S(2)}, u32[]{:S(2)}) async-start(bf16[8,24,128]{2,1,0:T(8,128)(2,1)} %shard_map.187), calls=%async_computation.2 | async-start | bytes 98304 | tf_op jit(solution)/shard_map/all_to_all | solution.py:485
  86.5 3.8 %collective-permute-start.10 = (bf16[192,128]{1,0:T(8,128)(2,1)S(1)}, bf16[192,128]{1,0:T(8,128)(2,1)S(1)}, u32[]{:S(2)}, u32[]{:S(2)}) collective-permute-start(bf16[192,128]{1,0:T(8,128)(2,1)S(1)} %bitcast.123), channel_id=1, source_target_pairs={{0,64},{64,0},{1,65},{65,1},{2,66},{66,2},{3,67},{67,3},{4,68},{68... | collective-permute-start | bytes 147464 | tf_op jit(solution)/shard_map/ppermute | solution.py:80
  94.2 11.2 %collective-permute-start.12 = (bf16[8,192,256]{2,1,0:T(8,128)(2,1)S(1)}, bf16[8,192,256]{2,1,0:T(8,128)(2,1)S(1)}, u32[]{:S(2)}, u32[]{:S(2)}) collective-permute-start(bf16[8,192,256]{2,1,0:T(8,128)(2,1)S(1)} %get-tuple-element.28), channel_id=1, source_target_pairs={{0,48},{2,50},{4,52},{6,54},{8,56},{10,58},{12,60},{14,62},{16,0},... | collective-permute-start | bytes 2359304 | tf_op jit(solution)/shard_map/ppermute | solution.py:43
  95.2 20.8 %collective-permute-start.13 = (bf16[8,192,256]{2,1,0:T(8,128)(2,1)S(1)}, bf16[8,192,256]{2,1,0:T(8,128)(2,1)S(1)}, u32[]{:S(2)}, u32[]{:S(2)}) collective-permute-start(bf16[8,192,256]{2,1,0:T(8,128)(2,1)S(1)} %get-tuple-element.29), channel_id=1, source_target_pairs={{0,16},{2,18},{4,20},{6,22},{8,24},{10,26},{12,28},{14,30},{16,32}... | collective-permute-start | bytes 2359304 | tf_op jit(solution)/shard_map/ppermute | solution.py:43
  95.8 20.2 %collective-permute-start.14 = (bf16[8,192,256]{2,1,0:T(8,128)(2,1)S(1)}, bf16[8,192,256]{2,1,0:T(8,128)(2,1)S(1)}, u32[]{:S(2)}, u32[]{:S(2)}) collective-permute-start(bf16[8,192,256]{2,1,0:T(8,128)(2,1)S(1)} %get-tuple-element.30), channel_id=1, source_target_pairs={{0,32},{2,34},{4,36},{6,38},{8,40},{10,42},{12,44},{14,46},{16,48}... | collective-permute-start | bytes 2359304 | tf_op jit(solution)/shard_map/ppermute | solution.py:43
  116.5 7.6 %collective-permute-start.15 = (bf16[2,192,256]{2,1,0:T(8,128)(2,1)S(1)}, bf16[2,192,256]{2,1,0:T(8,128)(2,1)S(1)}, u32[]{:S(2)}, u32[]{:S(2)}) collective-permute-start(bf16[2,192,256]{2,1,0:T(8,128)(2,1)S(1)} %get-tuple-element.50), channel_id=1, source_target_pairs={{0,6},{2,0},{4,2},{6,4},{8,14},{10,8},{12,10},{14,12},{16,22},{18,... | collective-permute-start | bytes 589832 | tf_op jit(solution)/shard_map/ppermute | solution.py:43
  118.6 8.1 %collective-permute-start.16 = (bf16[2,192,256]{2,1,0:T(8,128)(2,1)S(1)}, bf16[2,192,256]{2,1,0:T(8,128)(2,1)S(1)}, u32[]{:S(2)}, u32[]{:S(2)}) collective-permute-start(bf16[2,192,256]{2,1,0:T(8,128)(2,1)S(1)} %get-tuple-element.52), channel_id=1, source_target_pairs={{0,2},{2,4},{4,6},{6,0},{8,10},{10,12},{12,14},{14,8},{16,18},{18,... | collective-permute-start | bytes 589832 | tf_op jit(solution)/shard_map/ppermute | solution.py:43
  118.6 8.1 %collective-permute-start.17 = (bf16[2,192,256]{2,1,0:T(8,128)(2,1)S(1)}, bf16[2,192,256]{2,1,0:T(8,128)(2,1)S(1)}, u32[]{:S(2)}, u32[]{:S(2)}) collective-permute-start(bf16[2,192,256]{2,1,0:T(8,128)(2,1)S(1)} %get-tuple-element.51), channel_id=1, source_target_pairs={{0,4},{2,6},{4,0},{6,2},{8,12},{10,14},{12,8},{14,10},{16,20},{18,... | collective-permute-start | bytes 589832 | tf_op jit(solution)/shard_map/ppermute | solution.py:43
  121.4 24.8 %collective-permute-start.26 = (bf16[256,4096]{1,0:T(8,128)(2,1)}, bf16[256,4096]{1,0:T(8,128)(2,1)}, u32[]{:S(2)}, u32[]{:S(2)}) collective-permute-start(bf16[256,4096]{1,0:T(8,128)(2,1)} %constant_dynamic-slice_fusion), channel_id=1, source_target_pairs={{0,64},{64,0},{1,65},{65,1},{2,66},{66,2},{3,67},{67,3},{4,68},{68... | collective-permute-start | bytes 6291464 | tf_op jit(solution)/shard_map/ppermute | solution.py:80
  126.8 3.5 %collective-permute-start.18 = (bf16[192,256]{1,0:T(8,128)(2,1)S(1)}, bf16[192,256]{1,0:T(8,128)(2,1)S(1)}, u32[]{:S(2)}, u32[]{:S(2)}) collective-permute-start(bf16[192,256]{1,0:T(8,128)(2,1)S(1)} %fusion.20), channel_id=1, source_target_pairs={{0,8},{2,10},{4,12},{6,14},{8,0},{10,2},{12,4},{14,6},{16,24},{18,... | collective-permute-start | bytes 294920 | tf_op jit(solution)/shard_map/ppermute | solution.py:43
  130.4 4.1 %collective-permute-start.19 = (bf16[192,256]{1,0:T(8,128)(2,1)S(1)}, bf16[192,256]{1,0:T(8,128)(2,1)S(1)}, u32[]{:S(2)}, u32[]{:S(2)}) collective-permute-start(bf16[192,256]{1,0:T(8,128)(2,1)S(1)} %get-tuple-element.47), channel_id=1, source_target_pairs={{0,8},{2,10},{4,12},{6,14},{8,0},{10,2},{12,4},{14,6},{16,24},{18,... | collective-permute-start | bytes 294920 | tf_op jit(solution)/shard_map/ppermute | solution.py:43
  134.6 5.8 %collective-permute-start.20 = (bf16[2,192,256]{2,1,0:T(8,128)(2,1)S(1)}, bf16[2,192,256]{2,1,0:T(8,128)(2,1)S(1)}, u32[]{:S(2)}, u32[]{:S(2)}) collective-permute-start(bf16[2,192,256]{2,1,0:T(8,128)(2,1)S(1)} %pad_maximum_fusion.1), channel_id=1, source_target_pairs={{0,2},{2,4},{4,6},{6,0},{8,10},{10,12},{12,14},{14,8},{16,18},{18,... | collective-permute-start | bytes 589832 | tf_op jit(solution)/shard_map/ppermute | solution.py:43
  134.7 7.4 %collective-permute-start.21 = (bf16[2,192,256]{2,1,0:T(8,128)(2,1)S(1)}, bf16[2,192,256]{2,1,0:T(8,128)(2,1)S(1)}, u32[]{:S(2)}, u32[]{:S(2)}) collective-permute-start(bf16[2,192,256]{2,1,0:T(8,128)(2,1)S(1)} %pad_maximum_fusion.1), channel_id=1, source_target_pairs={{0,6},{2,0},{4,2},{6,4},{8,14},{10,8},{12,10},{14,12},{16,22},{18,... | collective-permute-start | bytes 589832 | tf_op jit(solution)/shard_map/ppermute | solution.py:43
  137.4 6.0 %collective-permute-start.22 = (bf16[2,192,256]{2,1,0:T(8,128)(2,1)S(1)}, bf16[2,192,256]{2,1,0:T(8,128)(2,1)S(1)}, u32[]{:S(2)}, u32[]{:S(2)}) collective-permute-start(bf16[2,192,256]{2,1,0:T(8,128)(2,1)S(1)} %pad_maximum_fusion.1), channel_id=1, source_target_pairs={{0,4},{2,6},{4,0},{6,2},{8,12},{10,14},{12,8},{14,10},{16,20},{18,... | collective-permute-start | bytes 589832 | tf_op jit(solution)/shard_map/ppermute | solution.py:43
  143.4 22.9 %collective-permute-start.23 = (bf16[8,192,256]{2,1,0:T(8,128)(2,1)S(1)}, bf16[8,192,256]{2,1,0:T(8,128)(2,1)S(1)}, u32[]{:S(2)}, u32[]{:S(2)}) collective-permute-start(bf16[8,192,256]{2,1,0:T(8,128)(2,1)S(1)} %constant_dynamic-update-slice_fusion.5.refs_0_), channel_id=1, source_target_pairs={{0,16},{2,18},{4,20},{6,22},{8,24},{10,26},{12,28},{14,30},{16,32}... | collective-permute-start | bytes 2359304 | tf_op jit(solution)/shard_map/ppermute | solution.py:43
  143.5 22.9 %collective-permute-start.24 = (bf16[8,192,256]{2,1,0:T(8,128)(2,1)S(1)}, bf16[8,192,256]{2,1,0:T(8,128)(2,1)S(1)}, u32[]{:S(2)}, u32[]{:S(2)}) collective-permute-start(bf16[8,192,256]{2,1,0:T(8,128)(2,1)S(1)} %constant_dynamic-update-slice_fusion.5.refs_0_), channel_id=1, source_target_pairs={{0,48},{2,50},{4,52},{6,54},{8,56},{10,58},{12,60},{14,62},{16,0},... | collective-permute-start | bytes 2359304 | tf_op jit(solution)/shard_map/ppermute | solution.py:43
  146.1 20.2 %collective-permute-start.25 = (bf16[8,192,256]{2,1,0:T(8,128)(2,1)S(1)}, bf16[8,192,256]{2,1,0:T(8,128)(2,1)S(1)}, u32[]{:S(2)}, u32[]{:S(2)}) collective-permute-start(bf16[8,192,256]{2,1,0:T(8,128)(2,1)S(1)} %constant_dynamic-update-slice_fusion.5.refs_0_), channel_id=1, source_target_pairs={{0,32},{2,34},{4,36},{6,38},{8,40},{10,42},{12,44},{14,46},{16,48}... | collective-permute-start | bytes 2359304 | tf_op jit(solution)/shard_map/ppermute | solution.py:43
  173.3 11.4 %collective-permute-start.28 = (f32[192,128]{1,0:T(8,128)}, f32[192,128]{1,0:T(8,128)}, u32[]{:S(2)}, u32[]{:S(2)}) collective-permute-start(f32[192,128]{1,0:T(8,128)} %get-tuple-element.33), channel_id=1, source_target_pairs={{0,64},{64,0},{1,65},{65,1},{2,66},{66,2},{3,67},{67,3},{4,68},{68... | collective-permute-start | bytes 294920 | tf_op jit(solution)/shard_map/ppermute | solution.py:80
  181.0 4.8 %collective-permute-start.27 = (f32[192,256]{1,0:T(8,128)}, f32[192,256]{1,0:T(8,128)}, u32[]{:S(2)}, u32[]{:S(2)}) collective-permute-start(f32[192,256]{1,0:T(8,128)} %get-tuple-element.32), channel_id=1, source_target_pairs={{0,64},{64,0},{1,65},{65,1},{2,66},{66,2},{3,67},{67,3},{4,68},{68... | collective-permute-start | bytes 589832 | tf_op jit(solution)/shard_map/ppermute | solution.py:80
  (26 other events, 179.9 us)
